TPU v7x, 32 devices: a whole 2x2x4 slice. The times are simulated.
32 devices in a mesh: gx: 8 (over z, x), gy: 4 (over y, core).
Axes of the slice: x: 2, y: 2, z: 4, core: 2. Of those that a mesh axis runs over, the one named last changes fastest.
Arguments:
- labels: int32 [48, 32, 256], P('gx', 'gy'), may hold values from 0 to 7
- permittivity_real: float32 [8], replicated, may hold values from 1 to 2.5
- permittivity_imag: float32 [8], replicated, may hold values from 0 to 0.5
- angles: float32 [360], replicated, may hold values from -3.140625 to 3.140625
- angle_pick: int32 [4], replicated, may hold values from 0 to 359
Outputs:
- scattered_field: float32 [2, 4, 48, 32, 256], P(None, None, 'gx', 'gy')
All inputs are finite; a program needn't handle non-finite values.
Results may differ from a plain program's by a relative error of at most 0.000054.
Values sent between devices are 32-bit elements; how exact they have to be, the bound alone decides.
A program may use at most 64 MiB of HBM per device.

v0:
```python
import jax
import jax.numpy as jnp
from jax import lax
from jax.sharding import PartitionSpec as P

NANG = 360
MAT = 8
COARSE_SWEEPS = 4


WEIGHTS = (128.0, -14.0, -3.0, -1.0)
DAMPING = 0.8
WAVE_SQUARED = 0.1
SHIFT_IMAG = 0.5
SOURCE_GAIN = 4.0


def with_halo(cells, sides, width):
    for axis, dim in sides:
        count = lax.axis_size(axis)
        ends = count - 1
        head = lax.slice_in_dim(cells, 0, width, axis=dim)
        tail = lax.slice_in_dim(cells, cells.shape[dim] - width, cells.shape[dim], axis=dim)
        cells = jnp.concatenate(
            [
                lax.ppermute(tail, axis, [(i, (i + 1) % count) for i in range(ends)]),
                cells,
                lax.ppermute(head, axis, [((i + 1) % count, i) for i in range(ends)]),
            ],
            axis=dim,
        )
    return cells


def shifted(shard, axis, by):
    size = lax.axis_size(axis)
    pairs = [(i, i + by) for i in range(size) if 0 <= i + by < size]
    return lax.ppermute(shard, axis, pairs)


def stencil(padded):
    extent_x = padded.shape[-3] - 2
    extent_y = padded.shape[-2] - 2
    extent_z = padded.shape[-1] - 2
    summed = jnp.zeros(padded.shape[:-3] + (extent_x, extent_y, extent_z), padded.dtype)
    for offset_x in (0, 1, 2):
        for offset_y in (0, 1, 2):
            for offset_z in (0, 1, 2):
                weight = WEIGHTS[abs(offset_x - 1) + abs(offset_y - 1) + abs(offset_z - 1)]
                summed = (
                    summed
                    + weight
                    * padded[
                        ...,
                        offset_x : offset_x + extent_x,
                        offset_y : offset_y + extent_y,
                        offset_z : offset_z + extent_z,
                    ]
                )
    return summed / 30.0


def complex_product(coefs, values):
    real_out = coefs[0] * values[0] - coefs[1] * values[1]
    imag_out = coefs[0] * values[1] + coefs[1] * values[0]
    return jnp.stack([real_out, imag_out])


def apply_operator(iterate, padded, medium, factor):
    laplace = stencil(padded) * factor
    return laplace - complex_product(medium, iterate)


def inverse_diagonal(medium, centre_weight):
    diag_real = centre_weight - medium[0]
    diag_imag = -medium[1]
    modulus = diag_real * diag_real + diag_imag * diag_imag
    return jnp.stack([diag_real / modulus, -diag_imag / modulus])


def restrict_axis(values, along):
    planes = (values.shape[along] - 1) // 2
    low_side = lax.slice_in_dim(values, 0, 2 * planes, 2, along)
    centre = lax.slice_in_dim(values, 1, 2 * planes, 2, along)
    high_side = lax.slice_in_dim(values, 2, 2 * planes + 1, 2, along)
    return (low_side + 2.0 * centre + high_side) * 0.25


def prolong_axis(values, along):
    planes = values.shape[along] - 1
    lower_part = lax.slice_in_dim(values, 0, planes, 1, along)
    upper_part = lax.slice_in_dim(values, 1, planes + 1, 1, along)
    even_rows = (lower_part + upper_part) * 0.5
    stacked = jnp.stack([even_rows, upper_part], axis=along + 1)
    new_shape = list(values.shape)
    new_shape[along] = 2 * planes
    return stacked.reshape(new_shape)


def fine_padded(iterate):
    padded = with_halo(iterate, (("gx", 2), ("gy", 3)), 1)
    return jnp.pad(padded, ((0, 0), (0, 0), (0, 0), (0, 0), (1, 1)))


def coarse_padded(correction):
    padded = with_halo(correction, (("gx", 2), ("gy", 3)), 1)
    return jnp.pad(padded, ((0, 0), (0, 0), (0, 0), (0, 0), (1, 1)))


def local(labels, permittivity_real, permittivity_imag, angles, angle_pick):
    cells_x, cells_y, cells_z = labels.shape
    eps_real = jnp.zeros(labels.shape, jnp.float32)
    eps_imag = jnp.zeros(labels.shape, jnp.float32)
    for material in range(MAT):
        chosen = labels == material
        eps_real = jnp.where(chosen, permittivity_real[material], eps_real)
        eps_imag = jnp.where(chosen, permittivity_imag[material], eps_imag)
    medium = WAVE_SQUARED * jnp.stack(
        [eps_real + SHIFT_IMAG * eps_imag, eps_imag - SHIFT_IMAG * eps_real]
    )
    pick_table = (angle_pick[:, None] == jnp.arange(NANG, dtype=jnp.int32)[None, :]).astype(
        jnp.float32
    )
    incidence = jnp.sum(pick_table * angles[None, :], axis=1)
    wavenumber = jnp.sqrt(WAVE_SQUARED)
    first_x = lax.axis_index("gx") * cells_x
    first_y = lax.axis_index("gy") * cells_y
    pos_x = (first_x + jnp.arange(cells_x, dtype=jnp.int32)).astype(jnp.float32)
    pos_y = (first_y + jnp.arange(cells_y, dtype=jnp.int32)).astype(jnp.float32)
    phases = wavenumber * (
        jnp.cos(incidence)[:, None, None] * pos_x[None, :, None]
        + jnp.sin(incidence)[:, None, None] * pos_y[None, None, :]
    )
    phases = phases[..., None]
    contrast = eps_real - 1.0
    source = SOURCE_GAIN * jnp.stack(
        [
            contrast * jnp.cos(phases) - eps_imag * jnp.sin(phases),
            contrast * jnp.sin(phases) + eps_imag * jnp.cos(phases),
        ]
    )
    inverse = inverse_diagonal(medium, 128.0 / 30.0)
    iterate = DAMPING * complex_product(inverse, source)
    residual = source - apply_operator(iterate, fine_padded(iterate), medium, 1.0)
    iterate = iterate + DAMPING * complex_product(inverse, residual)
    residual = source - apply_operator(iterate, fine_padded(iterate), medium, 1.0)
    rim_x = shifted(residual[:, :, :1], "gx", -1)
    extended = jnp.concatenate([residual, rim_x], axis=2)
    rim_y = shifted(extended[:, :, :, :1], "gy", -1)
    extended = jnp.concatenate([extended, rim_y], axis=3)
    extended = jnp.pad(extended, ((0, 0), (0, 0), (0, 0), (0, 0), (0, 1)))
    coarse_rhs = restrict_axis(restrict_axis(restrict_axis(extended, 2), 3), 4)
    coarse_medium = medium[:, 1::2, 1::2, 1::2]
    coarse_inverse = inverse_diagonal(coarse_medium, 128.0 / 120.0)
    correction = DAMPING * complex_product(coarse_inverse, coarse_rhs)
    for sweep_index in range(COARSE_SWEEPS - 1):
        coarse_res = coarse_rhs - apply_operator(
            correction, coarse_padded(correction), coarse_medium, 0.25
        )
        correction = correction + DAMPING * complex_product(coarse_inverse, coarse_res)
    rim_left = shifted(correction[:, :, -1:], "gx", 1)
    with_rim = jnp.concatenate([rim_left, correction], axis=2)
    rim_upper = shifted(with_rim[:, :, :, -1:], "gy", 1)
    with_rim = jnp.concatenate([rim_upper, with_rim], axis=3)
    with_rim = jnp.pad(with_rim, ((0, 0), (0, 0), (0, 0), (0, 0), (1, 0)))
    fine_correction = prolong_axis(prolong_axis(prolong_axis(with_rim, 2), 3), 4)
    return iterate + fine_correction


def solution(mesh):
    return jax.shard_map(
        local,
        mesh=mesh,
        in_specs=(P("gx", "gy", None), P(), P(), P(), P()),
        out_specs=P(None, None, "gx", "gy", None),
        check_vma=False,
    )
```

profile of v0, /device:TPU:1, one launch (start us, length us, event | category | flops | bytes accessed | tf_op | source)
XLA Modules:
  0.0 148.4 jit_solution(10274354187881198902)
XLA Ops:
  0.0 0.9 select_reduce_fusion
  0.9 1.6 %fusion.183 = (f32[1]{0:T(128)}, f32[1]{0:T(128)}, f32[1]{0:T(128)}, f32[1]{0:T(128)}, f32[1]{0:T(128)}, /*index=5*/f32[1]{0:T(128)}, f32[1]{0:T(128)}, f32[1]{0:T(128)}) fusion(f32[8]{0:T(128)} %param.6), kind=kLoop, calls=%fused_computation.446 | loop fusion | bytes 64 | tf_op jit(solution)/shard_map/slice | solution.py:116
  2.6 1.6 %fusion.182 = (f32[1]{0:T(128)}, f32[1]{0:T(128)}, f32[1]{0:T(128)}, f32[1]{0:T(128)}, f32[1]{0:T(128)}, /*index=5*/f32[1]{0:T(128)}, f32[1]{0:T(128)}, f32[1]{0:T(128)}) fusion(f32[8]{0:T(128)} %param.7), kind=kLoop, calls=%fused_computation.445 | loop fusion | bytes 64 | tf_op jit(solution)/shard_map/slice | solution.py:117
  4.2 0.9 broadcast_compare_fusion
  5.0 10.0 %add_bitcast_fusion = (f32[1,6,8,256]{3,2,1,0:T(8,128)S(1)}, f32[6,8,256]{2,1,0:T(8,128)S(1)}, f32[6,8,256]{2,1,0:T(8,128)S(1)}) fusion(pred[6,8,256]{2,1,0:T(8,128)(4,1)S(1)} %get-tuple-element.80, pred[6,8,256]{2,1,0:T(8,128)(4,1)S(1)} %get-tuple-element.79, pred[6,8,256]{2,1,0:T(8,128)(4,1)S(1)} %get-tuple-element.78, ...), kind=kLoop, calls=%fused_computation.383 | loop fusion | flops 221184 | bytes 245824 | tf_op jit(solution)/shard_map/stack | solution.py:118
  15.7 3.9 %collective-permute-start = (f32[2,4,1,8,256]{4,3,2,1,0:T(8,128)S(1)}, f32[2,4,1,8,256]{4,3,2,1,0:T(8,128)S(1)}, u32[]{:S(2)}, u32[]{:S(2)}) collective-permute-start(f32[2,4,1,8,256]{4,3,2,1,0:T(8,128)S(1)} %get-tuple-element.28), channel_id=1, source_target_pairs={{0,4},{4,8},{8,12},{12,16},{16,20},{20,24},{24,28},{1,5},{5,9},{9,... | collective-permute-start | bytes 196616 | tf_op jit(solution)/shard_map/ppermute | solution.py:26
  19.6 1.3 collective-permute-start.1
  20.9 3.7 %collective-permute-done.1 = f32[2,4,1,8,256]{4,3,2,1,0:T(8,128)S(1)} collective-permute-done((f32[2,4,1,8,256]{4,3,2,1,0:T(8,128)S(1)}, f32[2,4,1,8,256]{4,3,2,1,0:T(8,128)S(1)}, u32[]{:S(2)}, u32[]{:S(2)}) %collective-permute-start.1) | collective-permute-done | bytes 65568 | tf_op jit(solution)/shard_map/ppermute | solution.py:28
  24.8 4.0 %collective-permute-start.3 = (f32[2,4,8,1,256]{4,2,3,1,0:T(8,128)S(1)}, f32[2,4,8,1,256]{4,2,3,1,0:T(8,128)S(1)}, u32[]{:S(2)}, u32[]{:S(2)}) collective-permute-start(f32[2,4,8,1,256]{4,2,3,1,0:T(8,128)S(1)} %copy.365), channel_id=1, source_target_pairs={{1,0},{2,1},{3,2},{5,4},{6,5},{7,6},{9,8},{10,9},{11,10},{13,12},{... | collective-permute-start | bytes 196616 | tf_op jit(solution)/shard_map/ppermute | solution.py:28
  28.8 3.0 %collective-permute-start.2 = (f32[2,4,8,1,256]{4,2,3,1,0:T(8,128)S(1)}, f32[2,4,8,1,256]{4,2,3,1,0:T(8,128)S(1)}, u32[]{:S(2)}, u32[]{:S(2)}) collective-permute-start(f32[2,4,8,1,256]{4,2,3,1,0:T(8,128)S(1)} %copy.364), channel_id=1, source_target_pairs={{0,1},{1,2},{2,3},{4,5},{5,6},{6,7},{8,9},{9,10},{10,11},{12,13},{... | collective-permute-start | bytes 196616 | tf_op jit(solution)/shard_map/ppermute | solution.py:26
  32.0 1.2 collective-permute-done.2
  33.2 1.0 select_maximum_fusion.4
  34.2 0.3 maximum_maximum_fusion
  34.5 1.4 fusion.35
  36.0 4.1 %collective-permute-start.4 = (f32[2,4,1,8,256]{4,3,2,1,0:T(8,128)S(1)}, f32[2,4,1,8,256]{4,3,2,1,0:T(8,128)S(1)}, u32[]{:S(2)}, u32[]{:S(2)}) collective-permute-start(f32[2,4,1,8,256]{4,3,2,1,0:T(8,128)S(1)} %get-tuple-element.26), channel_id=1, source_target_pairs={{0,4},{4,8},{8,12},{12,16},{16,20},{20,24},{24,28},{1,5},{5,9},{9,... | collective-permute-start | bytes 196616 | tf_op jit(solution)/shard_map/ppermute | solution.py:26
  40.1 1.3 collective-permute-start.5
  41.4 1.4 slice.837
  42.8 2.7 %collective-permute-done.5 = f32[2,4,1,8,256]{4,3,2,1,0:T(8,128)S(1)} collective-permute-done((f32[2,4,1,8,256]{4,3,2,1,0:T(8,128)S(1)}, f32[2,4,1,8,256]{4,3,2,1,0:T(8,128)S(1)}, u32[]{:S(2)}, u32[]{:S(2)}) %collective-permute-start.5) | collective-permute-done | bytes 65568 | tf_op jit(solution)/shard_map/ppermute | solution.py:28
  45.6 2.3 %collective-permute-start.7 = (f32[2,4,8,1,256]{4,2,3,1,0:T(8,128)S(1)}, f32[2,4,8,1,256]{4,2,3,1,0:T(8,128)S(1)}, u32[]{:S(2)}, u32[]{:S(2)}) collective-permute-start(f32[2,4,8,1,256]{4,2,3,1,0:T(8,128)S(1)} %copy.371), channel_id=1, source_target_pairs={{1,0},{2,1},{3,2},{5,4},{6,5},{7,6},{9,8},{10,9},{11,10},{13,12},{... | collective-permute-start | bytes 196616 | tf_op jit(solution)/shard_map/ppermute | solution.py:28
  47.9 5.0 %collective-permute-start.6 = (f32[2,4,8,1,256]{4,2,3,1,0:T(8,128)S(1)}, f32[2,4,8,1,256]{4,2,3,1,0:T(8,128)S(1)}, u32[]{:S(2)}, u32[]{:S(2)}) collective-permute-start(f32[2,4,8,1,256]{4,2,3,1,0:T(8,128)S(1)} %copy.370), channel_id=1, source_target_pairs={{0,1},{1,2},{2,3},{4,5},{5,6},{6,7},{8,9},{9,10},{10,11},{12,13},{... | collective-permute-start | bytes 196616 | tf_op jit(solution)/shard_map/ppermute | solution.py:26
  53.0 1.2 collective-permute-done.6
  54.2 1.0 select_maximum_fusion
  55.2 0.3 maximum_maximum_fusion.1
  55.5 1.4 fusion.4
  56.9 1.3 collective-permute-start.8
  58.2 3.7 %collective-permute-done.8 = f32[2,4,1,8,256]{4,3,2,1,0:T(8,128)S(1)} collective-permute-done((f32[2,4,1,8,256]{4,3,2,1,0:T(8,128)S(1)}, f32[2,4,1,8,256]{4,3,2,1,0:T(8,128)S(1)}, u32[]{:S(2)}, u32[]{:S(2)}) %collective-permute-start.8) | collective-permute-done | bytes 65568 | tf_op jit(solution)/shard_map/ppermute | solution.py:38
  62.0 1.9 %collective-permute-start.9 = (f32[2,4,7,1,256]{4,1,3,2,0:T(4,128)S(1)}, f32[2,4,7,1,256]{4,1,3,2,0:T(4,128)S(1)}, u32[]{:S(2)}, u32[]{:S(2)}) collective-permute-start(f32[2,4,7,1,256]{4,1,3,2,0:T(4,128)S(1)} %copy.376), channel_id=1, source_target_pairs={{1,0},{2,1},{3,2},{5,4},{6,5},{7,6},{9,8},{10,9},{11,10},{13,12},{... | collective-permute-start | bytes 172040 | tf_op jit(solution)/shard_map/ppermute | solution.py:38
  64.0 0.2 copy.377
  64.2 5.1 %collective-permute-done.9 = f32[2,4,7,1,256]{4,1,3,2,0:T(4,128)S(1)} collective-permute-done((f32[2,4,7,1,256]{4,1,3,2,0:T(4,128)S(1)}, f32[2,4,7,1,256]{4,1,3,2,0:T(4,128)S(1)}, u32[]{:S(2)}, u32[]{:S(2)}) %collective-permute-start.9) | collective-permute-done | bytes 57376 | tf_op jit(solution)/shard_map/ppermute | solution.py:38
  69.6 2.2 %slice.882 = f32[2,4,3,4,128]{4,1,3,2,0:T(4,128)S(1)} slice(f32[2,4,3,4,257]{4,1,3,2,0:T(4,128)S(1)} %add_multiply_fusion.1), slice={[0:2:1], [0:4:1], [0:3:1], [0:4:1], [2:257:2]} | slice | bytes 98304 | tf_op jit(solution)/shard_map/slice | solution.py:85
  71.8 2.2 %slice.881 = f32[2,4,3,4,128]{4,1,3,2,0:T(4,128)S(1)} slice(f32[2,4,3,4,257]{4,1,3,2,0:T(4,128)S(1)} %add_multiply_fusion.1), slice={[0:2:1], [0:4:1], [0:3:1], [0:4:1], [1:256:2]} | slice | bytes 98304 | tf_op jit(solution)/shard_map/slice | solution.py:84
  74.0 2.2 %slice.880 = f32[2,4,3,4,128]{4,1,3,2,0:T(4,128)S(1)} slice(f32[2,4,3,4,257]{4,1,3,2,0:T(4,128)S(1)} %add_multiply_fusion.1), slice={[0:2:1], [0:4:1], [0:3:1], [0:4:1], [0:256:2]} | slice | bytes 98304 | tf_op jit(solution)/shard_map/slice | solution.py:83
  76.3 4.0 %collective-permute-start.10 = (f32[2,4,1,4,128]{4,1,3,2,0:T(4,128)S(1)}, f32[2,4,1,4,128]{4,1,3,2,0:T(4,128)S(1)}, u32[]{:S(2)}, u32[]{:S(2)}) collective-permute-start(f32[2,4,1,4,128]{4,1,3,2,0:T(4,128)S(1)} %get-tuple-element.70), channel_id=1, source_target_pairs={{0,4},{4,8},{8,12},{12,16},{16,20},{20,24},{24,28},{1,5},{5,9},{9,... | collective-permute-start | bytes 49160 | tf_op jit(solution)/shard_map/ppermute | solution.py:26
  80.3 1.3 collective-permute-start.11
  81.6 3.2 %collective-permute-done.11 = f32[2,4,1,4,128]{4,1,3,2,0:T(4,128)S(1)} collective-permute-done((f32[2,4,1,4,128]{4,1,3,2,0:T(4,128)S(1)}, f32[2,4,1,4,128]{4,1,3,2,0:T(4,128)S(1)}, u32[]{:S(2)}, u32[]{:S(2)}) %collective-permute-start.11) | collective-permute-done | bytes 16416 | tf_op jit(solution)/shard_map/ppermute | solution.py:28
  84.8 3.3 %collective-permute-start.12 = (f32[2,4,5,1,128]{4,1,3,2,0:T(4,128)S(1)}, f32[2,4,5,1,128]{4,1,3,2,0:T(4,128)S(1)}, u32[]{:S(2)}, u32[]{:S(2)}) collective-permute-start(f32[2,4,5,1,128]{4,1,3,2,0:T(4,128)S(1)} %get-tuple-element.50), channel_id=1, source_target_pairs={{0,1},{1,2},{2,3},{4,5},{5,6},{6,7},{8,9},{9,10},{10,11},{12,13},{... | collective-permute-start | bytes 61448 | tf_op jit(solution)/shard_map/ppermute | solution.py:26
  88.1 1.9 %collective-permute-start.13 = (f32[2,4,5,1,128]{4,1,3,2,0:T(4,128)S(1)}, f32[2,4,5,1,128]{4,1,3,2,0:T(4,128)S(1)}, u32[]{:S(2)}, u32[]{:S(2)}) collective-permute-start(f32[2,4,5,1,128]{4,1,3,2,0:T(4,128)S(1)} %get-tuple-element.51), channel_id=1, source_target_pairs={{1,0},{2,1},{3,2},{5,4},{6,5},{7,6},{9,8},{10,9},{11,10},{13,12},{... | collective-permute-start | bytes 61448 | tf_op jit(solution)/shard_map/ppermute | solution.py:28
  90.1 3.1 %collective-permute-done.13 = f32[2,4,5,1,128]{4,1,3,2,0:T(4,128)S(1)} collective-permute-done((f32[2,4,5,1,128]{4,1,3,2,0:T(4,128)S(1)}, f32[2,4,5,1,128]{4,1,3,2,0:T(4,128)S(1)}, u32[]{:S(2)}, u32[]{:S(2)}) %collective-permute-start.13) | collective-permute-done | bytes 20512 | tf_op jit(solution)/shard_map/ppermute | solution.py:28
  93.3 0.2 select_maximum_fusion.17
  93.5 0.3 fusion.138
  93.9 3.2 %collective-permute-start.14 = (f32[2,4,1,4,128]{4,1,3,2,0:T(4,128)S(1)}, f32[2,4,1,4,128]{4,1,3,2,0:T(4,128)S(1)}, u32[]{:S(2)}, u32[]{:S(2)}) collective-permute-start(f32[2,4,1,4,128]{4,1,3,2,0:T(4,128)S(1)} %get-tuple-element.68), channel_id=1, source_target_pairs={{0,4},{4,8},{8,12},{12,16},{16,20},{20,24},{24,28},{1,5},{5,9},{9,... | collective-permute-start | bytes 49160 | tf_op jit(solution)/shard_map/ppermute | solution.py:26
  97.1 1.3 collective-permute-start.15
  98.4 3.2 %collective-permute-done.15 = f32[2,4,1,4,128]{4,1,3,2,0:T(4,128)S(1)} collective-permute-done((f32[2,4,1,4,128]{4,1,3,2,0:T(4,128)S(1)}, f32[2,4,1,4,128]{4,1,3,2,0:T(4,128)S(1)}, u32[]{:S(2)}, u32[]{:S(2)}) %collective-permute-start.15) | collective-permute-done | bytes 16416 | tf_op jit(solution)/shard_map/ppermute | solution.py:28
  101.5 3.4 %collective-permute-start.16 = (f32[2,4,5,1,128]{4,1,3,2,0:T(4,128)S(1)}, f32[2,4,5,1,128]{4,1,3,2,0:T(4,128)S(1)}, u32[]{:S(2)}, u32[]{:S(2)}) collective-permute-start(f32[2,4,5,1,128]{4,1,3,2,0:T(4,128)S(1)} %get-tuple-element.46), channel_id=1, source_target_pairs={{0,1},{1,2},{2,3},{4,5},{5,6},{6,7},{8,9},{9,10},{10,11},{12,13},{... | collective-permute-start | bytes 61448 | tf_op jit(solution)/shard_map/ppermute | solution.py:26
  104.9 1.9 %collective-permute-start.17 = (f32[2,4,5,1,128]{4,1,3,2,0:T(4,128)S(1)}, f32[2,4,5,1,128]{4,1,3,2,0:T(4,128)S(1)}, u32[]{:S(2)}, u32[]{:S(2)}) collective-permute-start(f32[2,4,5,1,128]{4,1,3,2,0:T(4,128)S(1)} %get-tuple-element.47), channel_id=1, source_target_pairs={{1,0},{2,1},{3,2},{5,4},{6,5},{7,6},{9,8},{10,9},{11,10},{13,12},{... | collective-permute-start | bytes 61448 | tf_op jit(solution)/shard_map/ppermute | solution.py:28
  106.9 3.1 %collective-permute-done.17 = f32[2,4,5,1,128]{4,1,3,2,0:T(4,128)S(1)} collective-permute-done((f32[2,4,5,1,128]{4,1,3,2,0:T(4,128)S(1)}, f32[2,4,5,1,128]{4,1,3,2,0:T(4,128)S(1)}, u32[]{:S(2)}, u32[]{:S(2)}) %collective-permute-start.17) | collective-permute-done | bytes 20512 | tf_op jit(solution)/shard_map/ppermute | solution.py:28
  110.1 0.2 select_maximum_fusion.13
  110.3 0.3 fusion.107
  110.7 4.0 %collective-permute-start.18 = (f32[2,4,1,4,128]{4,1,3,2,0:T(4,128)S(1)}, f32[2,4,1,4,128]{4,1,3,2,0:T(4,128)S(1)}, u32[]{:S(2)}, u32[]{:S(2)}) collective-permute-start(f32[2,4,1,4,128]{4,1,3,2,0:T(4,128)S(1)} %get-tuple-element.66), channel_id=1, source_target_pairs={{0,4},{4,8},{8,12},{12,16},{16,20},{20,24},{24,28},{1,5},{5,9},{9,... | collective-permute-start | bytes 49160 | tf_op jit(solution)/shard_map/ppermute | solution.py:26
  114.7 1.3 collective-permute-start.19
  116.0 3.2 %collective-permute-done.19 = f32[2,4,1,4,128]{4,1,3,2,0:T(4,128)S(1)} collective-permute-done((f32[2,4,1,4,128]{4,1,3,2,0:T(4,128)S(1)}, f32[2,4,1,4,128]{4,1,3,2,0:T(4,128)S(1)}, u32[]{:S(2)}, u32[]{:S(2)}) %collective-permute-start.19) | collective-permute-done | bytes 16416 | tf_op jit(solution)/shard_map/ppermute | solution.py:28
  119.2 3.4 %collective-permute-start.20 = (f32[2,4,5,1,128]{4,1,3,2,0:T(4,128)S(1)}, f32[2,4,5,1,128]{4,1,3,2,0:T(4,128)S(1)}, u32[]{:S(2)}, u32[]{:S(2)}) collective-permute-start(f32[2,4,5,1,128]{4,1,3,2,0:T(4,128)S(1)} %get-tuple-element.42), channel_id=1, source_target_pairs={{0,1},{1,2},{2,3},{4,5},{5,6},{6,7},{8,9},{9,10},{10,11},{12,13},{... | collective-permute-start | bytes 61448 | tf_op jit(solution)/shard_map/ppermute | solution.py:26
  122.5 1.9 %collective-permute-start.21 = (f32[2,4,5,1,128]{4,1,3,2,0:T(4,128)S(1)}, f32[2,4,5,1,128]{4,1,3,2,0:T(4,128)S(1)}, u32[]{:S(2)}, u32[]{:S(2)}) collective-permute-start(f32[2,4,5,1,128]{4,1,3,2,0:T(4,128)S(1)} %get-tuple-element.43), channel_id=1, source_target_pairs={{1,0},{2,1},{3,2},{5,4},{6,5},{7,6},{9,8},{10,9},{11,10},{13,12},{... | collective-permute-start | bytes 61448 | tf_op jit(solution)/shard_map/ppermute | solution.py:28
  124.5 3.1 %collective-permute-done.21 = f32[2,4,5,1,128]{4,1,3,2,0:T(4,128)S(1)} collective-permute-done((f32[2,4,5,1,128]{4,1,3,2,0:T(4,128)S(1)}, f32[2,4,5,1,128]{4,1,3,2,0:T(4,128)S(1)}, u32[]{:S(2)}, u32[]{:S(2)}) %collective-permute-start.21) | collective-permute-done | bytes 20512 | tf_op jit(solution)/shard_map/ppermute | solution.py:28
  127.7 0.2 select_maximum_fusion.9
  127.9 0.3 fusion.76
  128.3 3.2 %collective-permute-start.22 = (f32[2,4,1,4,128]{4,1,3,2,0:T(4,128)S(1)}, f32[2,4,1,4,128]{4,1,3,2,0:T(4,128)S(1)}, u32[]{:S(2)}, u32[]{:S(2)}) collective-permute-start(f32[2,4,1,4,128]{4,1,3,2,0:T(4,128)S(1)} %slice.1154), channel_id=1, source_target_pairs={{0,4},{4,8},{8,12},{12,16},{16,20},{20,24},{24,28},{1,5},{5,9},{9,... | collective-permute-start | bytes 49160 | tf_op jit(solution)/shard_map/ppermute | solution.py:38
  131.5 0.9 collective-permute-done.22
  132.4 2.8 %collective-permute-start.23 = (f32[2,4,4,1,128]{4,2,3,1,0:T(4,128)S(1)}, f32[2,4,4,1,128]{4,2,3,1,0:T(4,128)S(1)}, u32[]{:S(2)}, u32[]{:S(2)}) collective-permute-start(f32[2,4,4,1,128]{4,2,3,1,0:T(4,128)S(1)} %copy.378), channel_id=1, source_target_pairs={{0,1},{1,2},{2,3},{4,5},{5,6},{6,7},{8,9},{9,10},{10,11},{12,13},{... | collective-permute-start | bytes 49160 | tf_op jit(solution)/shard_map/ppermute | solution.py:38
  135.2 0.8 collective-permute-done.23
  136.6 0.2 fusion.67
  136.9 6.4 %copy.385 = f32[2,4,6,8,128,2]{3,5,4,2,1,0:T(2,128)} copy(f32[2,4,6,8,128,2]{4,1,3,2,0,5:T(4,128)S(1)} %pad_maximum_fusion.9) | data formatting | bytes 786432 | tf_op jit(solution)/shard_map/stack | solution.py:94
  143.3 4.3 %copy.386 = f32[2,4,6,8,256]{4,3,2,1,0:T(8,128)S(1)} copy(f32[2,4,6,8,256]{3,4,2,1,0:T(8,128)} %bitcast.51) | data formatting | bytes 786432 | tf_op jit(solution)/shard_map/reshape | solution.py:97
  147.6 0.8 fusion.185
  (82 shorter events, 3.0 us)
Async XLA Ops:
  15.7 5.3 %collective-permute-start = (f32[2,4,1,8,256]{4,3,2,1,0:T(8,128)S(1)}, f32[2,4,1,8,256]{4,3,2,1,0:T(8,128)S(1)}, u32[]{:S(2)}, u32[]{:S(2)}) collective-permute-start(f32[2,4,1,8,256]{4,3,2,1,0:T(8,128)S(1)} %get-tuple-element.28), channel_id=1, source_target_pairs={{0,4},{4,8},{8,12},{12,16},{16,20},{20,24},{24,28},{1,5},{5,9},{9,... | collective-permute-start | bytes 196616 | tf_op jit(solution)/shard_map/ppermute | solution.py:26
  19.6 5.0 %collective-permute-start.1 = (f32[2,4,1,8,256]{4,3,2,1,0:T(8,128)S(1)}, f32[2,4,1,8,256]{4,3,2,1,0:T(8,128)S(1)}, u32[]{:S(2)}, u32[]{:S(2)}) collective-permute-start(f32[2,4,1,8,256]{4,3,2,1,0:T(8,128)S(1)} %get-tuple-element.29), channel_id=1, source_target_pairs={{4,0},{8,4},{12,8},{16,12},{20,16},{24,20},{28,24},{5,1},{9,5},{13... | collective-permute-start | bytes 196616 | tf_op jit(solution)/shard_map/ppermute | solution.py:28
  24.8 7.1 %collective-permute-start.3 = (f32[2,4,8,1,256]{4,2,3,1,0:T(8,128)S(1)}, f32[2,4,8,1,256]{4,2,3,1,0:T(8,128)S(1)}, u32[]{:S(2)}, u32[]{:S(2)}) collective-permute-start(f32[2,4,8,1,256]{4,2,3,1,0:T(8,128)S(1)} %copy.365), channel_id=1, source_target_pairs={{1,0},{2,1},{3,2},{5,4},{6,5},{7,6},{9,8},{10,9},{11,10},{13,12},{... | collective-permute-start | bytes 196616 | tf_op jit(solution)/shard_map/ppermute | solution.py:28
  28.8 4.4 %collective-permute-start.2 = (f32[2,4,8,1,256]{4,2,3,1,0:T(8,128)S(1)}, f32[2,4,8,1,256]{4,2,3,1,0:T(8,128)S(1)}, u32[]{:S(2)}, u32[]{:S(2)}) collective-permute-start(f32[2,4,8,1,256]{4,2,3,1,0:T(8,128)S(1)} %copy.364), channel_id=1, source_target_pairs={{0,1},{1,2},{2,3},{4,5},{5,6},{6,7},{8,9},{9,10},{10,11},{12,13},{... | collective-permute-start | bytes 196616 | tf_op jit(solution)/shard_map/ppermute | solution.py:26
  36.0 6.8 %collective-permute-start.4 = (f32[2,4,1,8,256]{4,3,2,1,0:T(8,128)S(1)}, f32[2,4,1,8,256]{4,3,2,1,0:T(8,128)S(1)}, u32[]{:S(2)}, u32[]{:S(2)}) collective-permute-start(f32[2,4,1,8,256]{4,3,2,1,0:T(8,128)S(1)} %get-tuple-element.26), channel_id=1, source_target_pairs={{0,4},{4,8},{8,12},{12,16},{16,20},{20,24},{24,28},{1,5},{5,9},{9,... | collective-permute-start | bytes 196616 | tf_op jit(solution)/shard_map/ppermute | solution.py:26
  40.1 5.4 %collective-permute-start.5 = (f32[2,4,1,8,256]{4,3,2,1,0:T(8,128)S(1)}, f32[2,4,1,8,256]{4,3,2,1,0:T(8,128)S(1)}, u32[]{:S(2)}, u32[]{:S(2)}) collective-permute-start(f32[2,4,1,8,256]{4,3,2,1,0:T(8,128)S(1)} %get-tuple-element.27), channel_id=1, source_target_pairs={{4,0},{8,4},{12,8},{16,12},{20,16},{24,20},{28,24},{5,1},{9,5},{13... | collective-permute-start | bytes 196616 | tf_op jit(solution)/shard_map/ppermute | solution.py:28
  45.6 7.3 %collective-permute-start.7 = (f32[2,4,8,1,256]{4,2,3,1,0:T(8,128)S(1)}, f32[2,4,8,1,256]{4,2,3,1,0:T(8,128)S(1)}, u32[]{:S(2)}, u32[]{:S(2)}) collective-permute-start(f32[2,4,8,1,256]{4,2,3,1,0:T(8,128)S(1)} %copy.371), channel_id=1, source_target_pairs={{1,0},{2,1},{3,2},{5,4},{6,5},{7,6},{9,8},{10,9},{11,10},{13,12},{... | collective-permute-start | bytes 196616 | tf_op jit(solution)/shard_map/ppermute | solution.py:28
  47.9 6.3 %collective-permute-start.6 = (f32[2,4,8,1,256]{4,2,3,1,0:T(8,128)S(1)}, f32[2,4,8,1,256]{4,2,3,1,0:T(8,128)S(1)}, u32[]{:S(2)}, u32[]{:S(2)}) collective-permute-start(f32[2,4,8,1,256]{4,2,3,1,0:T(8,128)S(1)} %copy.370), channel_id=1, source_target_pairs={{0,1},{1,2},{2,3},{4,5},{5,6},{6,7},{8,9},{9,10},{10,11},{12,13},{... | collective-permute-start | bytes 196616 | tf_op jit(solution)/shard_map/ppermute | solution.py:26
  56.9 5.0 %collective-permute-start.8 = (f32[2,4,1,8,256]{4,3,2,1,0:T(8,128)S(1)}, f32[2,4,1,8,256]{4,3,2,1,0:T(8,128)S(1)}, u32[]{:S(2)}, u32[]{:S(2)}) collective-permute-start(f32[2,4,1,8,256]{4,3,2,1,0:T(8,128)S(1)} %slice.1059), channel_id=1, source_target_pairs={{4,0},{8,4},{12,8},{16,12},{20,16},{24,20},{28,24},{5,1},{9,5},{13... | collective-permute-start | bytes 196616 | tf_op jit(solution)/shard_map/ppermute | solution.py:38
  62.0 7.3 %collective-permute-start.9 = (f32[2,4,7,1,256]{4,1,3,2,0:T(4,128)S(1)}, f32[2,4,7,1,256]{4,1,3,2,0:T(4,128)S(1)}, u32[]{:S(2)}, u32[]{:S(2)}) collective-permute-start(f32[2,4,7,1,256]{4,1,3,2,0:T(4,128)S(1)} %copy.376), channel_id=1, source_target_pairs={{1,0},{2,1},{3,2},{5,4},{6,5},{7,6},{9,8},{10,9},{11,10},{13,12},{... | collective-permute-start | bytes 172040 | tf_op jit(solution)/shard_map/ppermute | solution.py:38
  76.3 5.3 %collective-permute-start.10 = (f32[2,4,1,4,128]{4,1,3,2,0:T(4,128)S(1)}, f32[2,4,1,4,128]{4,1,3,2,0:T(4,128)S(1)}, u32[]{:S(2)}, u32[]{:S(2)}) collective-permute-start(f32[2,4,1,4,128]{4,1,3,2,0:T(4,128)S(1)} %get-tuple-element.70), channel_id=1, source_target_pairs={{0,4},{4,8},{8,12},{12,16},{16,20},{20,24},{24,28},{1,5},{5,9},{9,... | collective-permute-start | bytes 49160 | tf_op jit(solution)/shard_map/ppermute | solution.py:26
  80.3 4.5 %collective-permute-start.11 = (f32[2,4,1,4,128]{4,1,3,2,0:T(4,128)S(1)}, f32[2,4,1,4,128]{4,1,3,2,0:T(4,128)S(1)}, u32[]{:S(2)}, u32[]{:S(2)}) collective-permute-start(f32[2,4,1,4,128]{4,1,3,2,0:T(4,128)S(1)} %get-tuple-element.71), channel_id=1, source_target_pairs={{4,0},{8,4},{12,8},{16,12},{20,16},{24,20},{28,24},{5,1},{9,5},{13... | collective-permute-start | bytes 49160 | tf_op jit(solution)/shard_map/ppermute | solution.py:28
  84.8 5.3 %collective-permute-start.12 = (f32[2,4,5,1,128]{4,1,3,2,0:T(4,128)S(1)}, f32[2,4,5,1,128]{4,1,3,2,0:T(4,128)S(1)}, u32[]{:S(2)}, u32[]{:S(2)}) collective-permute-start(f32[2,4,5,1,128]{4,1,3,2,0:T(4,128)S(1)} %get-tuple-element.50), channel_id=1, source_target_pairs={{0,1},{1,2},{2,3},{4,5},{5,6},{6,7},{8,9},{9,10},{10,11},{12,13},{... | collective-permute-start | bytes 61448 | tf_op jit(solution)/shard_map/ppermute | solution.py:26
  88.1 5.1 %collective-permute-start.13 = (f32[2,4,5,1,128]{4,1,3,2,0:T(4,128)S(1)}, f32[2,4,5,1,128]{4,1,3,2,0:T(4,128)S(1)}, u32[]{:S(2)}, u32[]{:S(2)}) collective-permute-start(f32[2,4,5,1,128]{4,1,3,2,0:T(4,128)S(1)} %get-tuple-element.51), channel_id=1, source_target_pairs={{1,0},{2,1},{3,2},{5,4},{6,5},{7,6},{9,8},{10,9},{11,10},{13,12},{... | collective-permute-start | bytes 61448 | tf_op jit(solution)/shard_map/ppermute | solution.py:28
  93.9 4.5 %collective-permute-start.14 = (f32[2,4,1,4,128]{4,1,3,2,0:T(4,128)S(1)}, f32[2,4,1,4,128]{4,1,3,2,0:T(4,128)S(1)}, u32[]{:S(2)}, u32[]{:S(2)}) collective-permute-start(f32[2,4,1,4,128]{4,1,3,2,0:T(4,128)S(1)} %get-tuple-element.68), channel_id=1, source_target_pairs={{0,4},{4,8},{8,12},{12,16},{16,20},{20,24},{24,28},{1,5},{5,9},{9,... | collective-permute-start | bytes 49160 | tf_op jit(solution)/shard_map/ppermute | solution.py:26
  97.1 4.5 %collective-permute-start.15 = (f32[2,4,1,4,128]{4,1,3,2,0:T(4,128)S(1)}, f32[2,4,1,4,128]{4,1,3,2,0:T(4,128)S(1)}, u32[]{:S(2)}, u32[]{:S(2)}) collective-permute-start(f32[2,4,1,4,128]{4,1,3,2,0:T(4,128)S(1)} %get-tuple-element.69), channel_id=1, source_target_pairs={{4,0},{8,4},{12,8},{16,12},{20,16},{24,20},{28,24},{5,1},{9,5},{13... | collective-permute-start | bytes 49160 | tf_op jit(solution)/shard_map/ppermute | solution.py:28
  101.5 5.3 %collective-permute-start.16 = (f32[2,4,5,1,128]{4,1,3,2,0:T(4,128)S(1)}, f32[2,4,5,1,128]{4,1,3,2,0:T(4,128)S(1)}, u32[]{:S(2)}, u32[]{:S(2)}) collective-permute-start(f32[2,4,5,1,128]{4,1,3,2,0:T(4,128)S(1)} %get-tuple-element.46), channel_id=1, source_target_pairs={{0,1},{1,2},{2,3},{4,5},{5,6},{6,7},{8,9},{9,10},{10,11},{12,13},{... | collective-permute-start | bytes 61448 | tf_op jit(solution)/shard_map/ppermute | solution.py:26
  104.9 5.1 %collective-permute-start.17 = (f32[2,4,5,1,128]{4,1,3,2,0:T(4,128)S(1)}, f32[2,4,5,1,128]{4,1,3,2,0:T(4,128)S(1)}, u32[]{:S(2)}, u32[]{:S(2)}) collective-permute-start(f32[2,4,5,1,128]{4,1,3,2,0:T(4,128)S(1)} %get-tuple-element.47), channel_id=1, source_target_pairs={{1,0},{2,1},{3,2},{5,4},{6,5},{7,6},{9,8},{10,9},{11,10},{13,12},{... | collective-permute-start | bytes 61448 | tf_op jit(solution)/shard_map/ppermute | solution.py:28
  110.7 5.3 %collective-permute-start.18 = (f32[2,4,1,4,128]{4,1,3,2,0:T(4,128)S(1)}, f32[2,4,1,4,128]{4,1,3,2,0:T(4,128)S(1)}, u32[]{:S(2)}, u32[]{:S(2)}) collective-permute-start(f32[2,4,1,4,128]{4,1,3,2,0:T(4,128)S(1)} %get-tuple-element.66), channel_id=1, source_target_pairs={{0,4},{4,8},{8,12},{12,16},{16,20},{20,24},{24,28},{1,5},{5,9},{9,... | collective-permute-start | bytes 49160 | tf_op jit(solution)/shard_map/ppermute | solution.py:26
  114.7 4.5 %collective-permute-start.19 = (f32[2,4,1,4,128]{4,1,3,2,0:T(4,128)S(1)}, f32[2,4,1,4,128]{4,1,3,2,0:T(4,128)S(1)}, u32[]{:S(2)}, u32[]{:S(2)}) collective-permute-start(f32[2,4,1,4,128]{4,1,3,2,0:T(4,128)S(1)} %get-tuple-element.67), channel_id=1, source_target_pairs={{4,0},{8,4},{12,8},{16,12},{20,16},{24,20},{28,24},{5,1},{9,5},{13... | collective-permute-start | bytes 49160 | tf_op jit(solution)/shard_map/ppermute | solution.py:28
  119.2 5.3 %collective-permute-start.20 = (f32[2,4,5,1,128]{4,1,3,2,0:T(4,128)S(1)}, f32[2,4,5,1,128]{4,1,3,2,0:T(4,128)S(1)}, u32[]{:S(2)}, u32[]{:S(2)}) collective-permute-start(f32[2,4,5,1,128]{4,1,3,2,0:T(4,128)S(1)} %get-tuple-element.42), channel_id=1, source_target_pairs={{0,1},{1,2},{2,3},{4,5},{5,6},{6,7},{8,9},{9,10},{10,11},{12,13},{... | collective-permute-start | bytes 61448 | tf_op jit(solution)/shard_map/ppermute | solution.py:26
  122.5 5.1 %collective-permute-start.21 = (f32[2,4,5,1,128]{4,1,3,2,0:T(4,128)S(1)}, f32[2,4,5,1,128]{4,1,3,2,0:T(4,128)S(1)}, u32[]{:S(2)}, u32[]{:S(2)}) collective-permute-start(f32[2,4,5,1,128]{4,1,3,2,0:T(4,128)S(1)} %get-tuple-element.43), channel_id=1, source_target_pairs={{1,0},{2,1},{3,2},{5,4},{6,5},{7,6},{9,8},{10,9},{11,10},{13,12},{... | collective-permute-start | bytes 61448 | tf_op jit(solution)/shard_map/ppermute | solution.py:28
  128.3 4.0 %collective-permute-start.22 = (f32[2,4,1,4,128]{4,1,3,2,0:T(4,128)S(1)}, f32[2,4,1,4,128]{4,1,3,2,0:T(4,128)S(1)}, u32[]{:S(2)}, u32[]{:S(2)}) collective-permute-start(f32[2,4,1,4,128]{4,1,3,2,0:T(4,128)S(1)} %slice.1154), channel_id=1, source_target_pairs={{0,4},{4,8},{8,12},{12,16},{16,20},{20,24},{24,28},{1,5},{5,9},{9,... | collective-permute-start | bytes 49160 | tf_op jit(solution)/shard_map/ppermute | solution.py:38
  132.4 3.6 %collective-permute-start.23 = (f32[2,4,4,1,128]{4,2,3,1,0:T(4,128)S(1)}, f32[2,4,4,1,128]{4,2,3,1,0:T(4,128)S(1)}, u32[]{:S(2)}, u32[]{:S(2)}) collective-permute-start(f32[2,4,4,1,128]{4,2,3,1,0:T(4,128)S(1)} %copy.378), channel_id=1, source_target_pairs={{0,1},{1,2},{2,3},{4,5},{5,6},{6,7},{8,9},{9,10},{10,11},{12,13},{... | collective-permute-start | bytes 49160 | tf_op jit(solution)/shard_map/ppermute | solution.py:38
where the time goes:
time: 151 us; the launch traced here: 148 us
  starting transfers between devices  64.9 us (43%)
  waiting for transfers between devices  38.1 us (25%)
  local copies, waits for them, and re-layouts  22.6 us (15%)
  other arithmetic  21.9 us (15%)
    ppermute x10, starting transfers between devices, with_halo(): lax.ppermute(tail, axis, [(i, (i + 1) % count) for i in range(ends)])  37.3 us
    ppermute x10, waiting for transfers between devices, with_halo(): lax.ppermute(head, axis, [((i + 1) % count, i) for i in range(ends)])  25.3 us
    ppermute x10, starting transfers between devices, with_halo(): lax.ppermute(head, axis, [((i + 1) % count, i) for i in range(ends)])  18.5 us
    ppermute x4, waiting for transfers between devices, shifted(): return lax.ppermute(shard, axis, pairs)  10.4 us
    another operation x2, other arithmetic, local(): jnp.stack([eps_real + SHIFT_IMAG * eps_imag, eps_imag - SHIFT_IMAG * eps_...  9.99 us
    ppermute x4, starting transfers between devices, shifted(): return lax.ppermute(shard, axis, pairs)  9.17 us
    another operation x4, local copies, waits for them, and re-layouts, prolong_axis(): stacked = jnp.stack([even_rows, upper_part], axis=along + 1)  6.46 us
    reshape x1, local copies, waits for them, and re-layouts, prolong_axis(): return stacked.reshape(new_shape)  4.33 us
  transfers between devices with their start and end apart: 24, of which 14 were waited for; matrix products, arithmetic and copies ran while one was open for 1% of the time, Pallas kernels for 0%

commit v1 on v0

v1 whole, which is shorter than its diff:
```python
import functools

import jax
import jax.numpy as jnp
from jax import lax
from jax.experimental import pallas as pl
from jax.experimental.pallas import tpu as pltpu
from jax.sharding import PartitionSpec as P

MAT = 8
DAMPING = 0.8
WAVE_SQUARED = 0.1
SHIFT_IMAG = 0.5
SOURCE_GAIN = 4.0
CENTRE = 128.0 / 30.0
COARSE_CENTRE = 128.0 / 120.0
LOW, HIGH = 2, 3
DIRS = [(dx, dy) for dx in (-1, 0, 1) for dy in (-1, 0, 1) if (dx, dy) != (0, 0)]
f32 = jnp.float32


def windows(step, size, low, high):
    if step == 0:
        return low, low, size
    if step > 0:
        return size, 0, low
    return low, low + size, high


def shift_up(values, first):
    return jnp.where(first, 0.0, pltpu.roll(values, 1, 1))


def shift_down(values, last):
    return jnp.where(last, 0.0, pltpu.roll(values, values.shape[1] - 1, 1))


def plane_sums(centre, ends, y):
    side = ends[y] + (centre[y - 1] + centre[y + 1])
    diag = ends[y - 1] + ends[y + 1]
    return 14.0 * side + 3.0 * diag, 14.0 * centre[y] + (3.0 * side + diag)


def fine_neighbours(buf, x, rows, first, last):
    span = range(rows[0] - 1, rows[-1] + 2)
    halves = []
    for half in (0, 1):
        centre = {y: buf[x, y, half] for y in span}
        ends = {y: buf[x - 1, y, half] + buf[x + 1, y, half] for y in span}
        halves.append([plane_sums(centre, ends, y) for y in rows])
    for i, y in enumerate(rows):
        (in_even, out_even), (in_odd, out_odd) = halves[0][i], halves[1][i]
        yield (
            y,
            in_even + (out_odd + shift_up(out_odd, first)),
            in_odd + (out_even + shift_down(out_even, last)),
        )


def coarse_neighbours(buf, x, rows, first, last):
    span = range(rows[0] - 1, rows[-1] + 2)
    centre = {y: buf[x, y] for y in span}
    ends = {y: buf[x - 1, y] + buf[x + 1, y] for y in span}
    for y in rows:
        inner, outer = plane_sums(centre, ends, y)
        yield y, inner + (shift_up(outer, first) + shift_down(outer, last))


def cycle_kernel(
    nx, ny,
    labels_ref, eps_r_ref, eps_i_ref, angles_ref, pick_ref,
    iterate_ref, corr_ref,
    lab, tab, ctab, ewave, wave, it0, w, yz, c0, c1, c2,
    send_sems, recv_sems,
):
    sizex, sizey, sizez = labels_ref.shape
    nzc = sizez // 2
    cx, cy = sizex // 2, sizey // 2
    extx, exty = sizex + LOW + HIGH, sizey + LOW + HIGH
    px, py = lax.axis_index("gx"), lax.axis_index("gy")

    def there(dx, dy):
        ok = None
        for step, pos, count in ((dx, px, nx), (dy, py, ny)):
            if step:
                one = (pos > 0) if step < 0 else (pos < count - 1)
                ok = one if ok is None else jnp.logical_and(ok, one)
        return ok

    lab[...] = jnp.full(lab.shape, float(MAT), f32)
    c0[...] = jnp.zeros(c0.shape, f32)
    c2[...] = jnp.zeros(c2.shape, f32)
    barrier = pltpu.get_barrier_semaphore()
    for dx, dy in DIRS:
        @pl.when(there(dx, dy))
        def _():
            pl.semaphore_signal(
                barrier, inc=1, device_id=(px + dx, py + dy), device_id_type=pl.DeviceIdType.MESH
            )

    row = lax.broadcasted_iota(jnp.int32, (sizez, sizez), 0)
    col = lax.broadcasted_iota(jnp.int32, (sizez, sizez), 1)
    split = jnp.where(row == jnp.where(col < nzc, 2 * col, 2 * (col - nzc) + 1), 1.0, 0.0).astype(jnp.bfloat16)
    mine = labels_ref[...].astype(f32).reshape(sizex * sizey, sizez).astype(jnp.bfloat16)
    mine = jnp.dot(mine, split, preferred_element_type=f32)
    for x in range(sizex):
        for half in (0, 1):
            lab[x + LOW, pl.ds(2 * LOW + half, sizey, stride=2), :] = mine[
                x * sizey : (x + 1) * sizey, half * nzc : (half + 1) * nzc
            ]

    def exchange(phase, buf, sizes, low, high, fold):
        copies = []
        for d, (dx, dy) in enumerate(DIRS):
            fx, tx, lx = windows(dx, sizes[0], low, high)
            fy, ty, ly = windows(dy, sizes[1], low, high)
            out = pltpu.make_async_remote_copy(
                src_ref=buf.at[pl.ds(fx, lx), pl.ds(fold * fy, fold * ly)],
                dst_ref=buf.at[pl.ds(tx, lx), pl.ds(fold * ty, fold * ly)],
                send_sem=send_sems.at[phase, d],
                recv_sem=recv_sems.at[phase, d],
                device_id=(px + dx, py + dy),
                device_id_type=pl.DeviceIdType.MESH,
            )
            copies.append(out)
            pl.when(there(dx, dy))(out.start)
        return copies

    def finish(copies):
        for (dx, dy), copy in zip(DIRS, copies):
            pl.when(there(-dx, -dy))(copy.wait_recv)

    def finish_sends(copies):
        for (dx, dy), copy in zip(DIRS, copies):
            pl.when(there(dx, dy))(copy.wait_send)

    one = jnp.int32(1)
    besides_x = jnp.where(px > 0, one, 0) + jnp.where(px < nx - 1, one, 0)
    besides_y = jnp.where(py > 0, one, 0) + jnp.where(py < ny - 1, one, 0)
    pl.semaphore_wait(barrier, (besides_x + 1) * (besides_y + 1) - 1)
    sent_labels = exchange(0, lab, (sizex, sizey), LOW, HIGH, 2)

    lane = lax.broadcasted_iota(jnp.int32, (8, nzc), 1)
    field = lax.broadcasted_iota(jnp.int32, (8, nzc), 0)
    first, last = lane == 0, lane == nzc - 1
    imag = field >= 4
    sign = jnp.where(imag, 1.0, -1.0)
    column = field % 4
    incidence = jnp.zeros((8, nzc), f32)
    for c in range(4):
        incidence = jnp.where(column == c, angles_ref[pick_ref[c]], incidence)
    wavenumber = jnp.sqrt(jnp.full((8, nzc), WAVE_SQUARED, f32))
    on_x = lane < nzc // 2
    place = jnp.where(on_x, px * sizex - LOW + lane, py * sizey - LOW + lane - nzc // 2).astype(f32)
    arg = wavenumber * jnp.where(on_x, jnp.cos(incidence), jnp.sin(incidence)) * place
    cos_all, sin_all = jnp.cos(arg), jnp.sin(arg)
    one_all = jnp.where(imag, sin_all, cos_all)
    two_all = jnp.where(imag, cos_all, -sin_all)
    spread = lambda values, at: jnp.broadcast_to(values[:, at : at + 1], (8, nzc))
    for x in range(extx):
        ewave[x, 0] = spread(one_all, x)
        ewave[x, 1] = spread(two_all, x)
    along_y = [
        (spread(cos_all, nzc // 2 + y), spread(sin_all, nzc // 2 + y)) for y in range(exty)
    ]
    for y in range(exty):
        ewave[extx + y, 0], ewave[extx + y, 1] = along_y[y]

    def fill_wave(x, carry):
        wave_one, wave_two = ewave[x, 0], ewave[x, 1]
        for y in range(exty):
            cos_y, sin_y = ewave[extx + y, 0], ewave[extx + y, 1]
            wave[x, y, 0] = cos_y * wave_one + sin_y * wave_two
            wave[x, y, 1] = cos_y * wave_two - sin_y * wave_one
        return carry

    lax.fori_loop(0, extx, fill_wave, 0)
    eps_table = [(eps_r_ref[m], eps_i_ref[m]) for m in range(MAT)]
    finish(sent_labels)

    def media(label):
        eps_r = jnp.zeros(label.shape, f32)
        eps_i = jnp.zeros(label.shape, f32)
        for m in range(MAT):
            chosen = label == float(m)
            eps_r = jnp.where(chosen, eps_table[m][0], eps_r)
            eps_i = jnp.where(chosen, eps_table[m][1], eps_i)
        med_r = WAVE_SQUARED * (eps_r + SHIFT_IMAG * eps_i)
        med_i = WAVE_SQUARED * (eps_i - SHIFT_IMAG * eps_r)
        return label < MAT - 0.5, eps_r, eps_i, med_r, med_i

    def damped_inverse(inside, med_r, med_i, centre):
        diag = centre - med_r
        scale = jnp.where(inside, DAMPING / (diag * diag + med_i * med_i), 0.0)
        return diag * scale, med_i * scale

    def bcast(ref, at):
        return jnp.broadcast_to(ref[at], (8, nzc))

    def fill_start(x, carry):
        inside, eps_r, eps_i, med_r, med_i = media(lab[x])
        inv_r, inv_i = damped_inverse(inside, med_r, med_i, CENTRE)
        src_r = jnp.where(inside, SOURCE_GAIN * (eps_r - 1.0), 0.0)
        src_i = SOURCE_GAIN * eps_i
        tab[0, x] = inv_r * src_r - inv_i * src_i
        tab[1, x] = inv_r * src_i + inv_i * src_r
        tab[2, x] = inv_r * (1.0 / 30.0)
        tab[3, x] = inv_i * (1.0 / 30.0)
        tab[4, x] = (0.2 * (1.0 - DAMPING)) * src_r
        tab[5, x] = (0.2 * (1.0 - DAMPING)) * src_i
        for y in range(exty):
            wave_one, wave_two = wave[x, y, 0], wave[x, y, 1]
            for half in (0, 1):
                at = (x, pl.ds(2 * y + half, 1))
                it0[x, y, half] = bcast(tab, (0, *at)) * wave_one + bcast(tab, (1, *at)) * wave_two
        return carry

    lax.fori_loop(0, extx, fill_start, 0)

    def fill_coarse_table(i, carry):
        inside, _, _, med_r, med_i = media(lab[2 * i + LOW - 1])
        ctab[0, i], ctab[1, i] = damped_inverse(inside, med_r, med_i, COARSE_CENTRE)
        return carry

    lax.fori_loop(0, cx + 2, fill_coarse_table, 0)

    def times(real, imaginary, values):
        return real * values + imaginary * (sign * pltpu.roll(values, 4, 0))

    def sweep(x, carry):
        for y, even, odd in fine_neighbours(it0, x, range(1, exty - 1), first, last):
            for half, near in enumerate((even, odd)):
                at = (x, pl.ds(2 * y + half, 1))
                change = times(bcast(tab, (2, *at)), bcast(tab, (3, *at)), near)
                w[x, y, half] = (1.0 + 0.2 - DAMPING) * it0[x, y, half] + change
        return carry

    lax.fori_loop(1, extx - 1, sweep, 0)

    def iterate_out(x, carry):
        for y in range(sizey):
            for half in (0, 1):
                iterate_ref[x, y, half] = w[x + LOW, y + LOW, half] + DAMPING * it0[x + LOW, y + LOW, half]
        return carry

    lax.fori_loop(0, sizex, iterate_out, 0)

    def restrict(x, carry):
        in_x = jnp.where(jnp.logical_and(x == LOW + sizex, px == nx - 1), 0.0, 1.0 / 30.0)
        in_xy = jnp.where(py == ny - 1, 0.0, in_x)
        rows = []
        for y, even, odd in fine_neighbours(w, x, range(LOW, LOW + sizey + 1), first, last):
            wave_one, wave_two = wave[x, y, 0], wave[x, y, 1]
            scale = in_xy if y == LOW + sizey else in_x
            both = []
            for half, near in enumerate((even, odd)):
                at = (x, pl.ds(2 * y + half, 1))
                both.append(
                    bcast(tab, (4, *at)) * wave_one + bcast(tab, (5, *at)) * wave_two + scale * near
                )
            rows.append(both)
        for j in range(cy):
            even, odd = (
                (rows[2 * j][half] + rows[2 * j + 2][half]) + 2.0 * rows[2 * j + 1][half]
                for half in (0, 1)
            )
            yz[x - LOW, j] = (even + shift_down(even, last)) + 2.0 * odd
        return carry

    lax.fori_loop(LOW, LOW + sizex + 1, restrict, 0)

    def coarse_inverse(i, j):
        at = (i - 1, pl.ds(2 * (2 * (j - 2) + 1 + LOW) + 1, 1))
        return bcast(ctab, (0, *at)), bcast(ctab, (1, *at))

    def first_correction(i, carry):
        for j in range(cy):
            rhs = (yz[2 * i, j] + yz[2 * i + 2, j]) + 2.0 * yz[2 * i + 1, j]
            c0[i + 2, j + 2] = times(*coarse_inverse(i + 2, j + 2), rhs * (1.0 / 64.0))
        return carry

    lax.fori_loop(0, cx, first_correction, 0)
    sent_first = exchange(1, c0, (cx, cy), 2, 2, 1)
    finish(sent_first)

    def coarse_sweep(source, put, i_range, j_range):
        def body(i, carry):
            for j, near in coarse_neighbours(source, i, j_range, first, last):
                change = times(*coarse_inverse(i, j), near * (1.0 / 120.0))
                put(i, j, (1.0 - DAMPING) * source[i, j] + c0[i, j] + change)
            return carry

        lax.fori_loop(*i_range, body, 0)

    def into(ref, off):
        def put(i, j, values):
            ref[i - off, j - off] = values

        return put

    coarse_sweep(c0, into(c1, 0), (1, cx + 3), range(1, cy + 3))
    coarse_sweep(c1, into(c2, 0), (2, cx + 2), range(2, cy + 2))
    sent_third = exchange(2, c2, (cx, cy), 2, 1, 1)
    finish(sent_third)
    coarse_sweep(c2, into(corr_ref, 1), (1, cx + 2), range(1, cy + 2))
    for sent in (sent_labels, sent_first, sent_third):
        finish_sends(sent)


def prolong_kernel(iterate_ref, corr_ref, out_ref, flat):
    sizex, sizey = iterate_ref.shape[:2]
    nzc = iterate_ref.shape[-1]
    sizez = 2 * nzc
    lane = lax.broadcasted_iota(jnp.int32, (8, nzc), 1)
    first = lane == 0
    row = lax.broadcasted_iota(jnp.int32, (sizez, sizez), 0)
    col = lax.broadcasted_iota(jnp.int32, (sizez, sizez), 1)
    merge = jnp.where(col == jnp.where(row < nzc, 2 * row, 2 * (row - nzc) + 1), 1.0, 0.0).astype(jnp.bfloat16)

    for x in range(sizex):
        i = x // 2 + 1
        across = {}
        for j in range(sizey // 2 + 1):
            across[j] = corr_ref[i, j] if x % 2 else (corr_ref[i - 1, j] + corr_ref[i, j]) * 0.5
        rows = []
        for y in range(sizey):
            j = y // 2 + 1
            odd = across[j] if y % 2 else (across[j - 1] + across[j]) * 0.5
            even = (odd + shift_up(odd, first)) * 0.5
            rows.append(
                jnp.concatenate([iterate_ref[x, y, 0] + even, iterate_ref[x, y, 1] + odd], axis=1)
            )
        block = jnp.concatenate(rows, axis=0)
        top = block.astype(jnp.bfloat16)
        rest = block - top.astype(f32)
        mid = rest.astype(jnp.bfloat16)
        tail = (rest - mid.astype(f32)).astype(jnp.bfloat16)
        merged = (
            jnp.dot(tail, merge, preferred_element_type=f32)
            + jnp.dot(mid, merge, preferred_element_type=f32)
            + jnp.dot(top, merge, preferred_element_type=f32)
        )
        for half in (0, 1):
            flat[x, half] = merged[:, half * nzc : (half + 1) * nzc]
        for f in range(8):
            for half in (0, 1):
                out_ref[f // 4, f % 4, x, :, half * nzc : (half + 1) * nzc] = flat[
                    x, half, pl.ds(f, sizey, stride=8), :
                ]


def local(nx, ny, labels, eps_r, eps_i, angles, pick):
    sizex, sizey, sizez = labels.shape
    nzc = sizez // 2
    cx, cy = sizex // 2, sizey // 2
    extx, exty = sizex + LOW + HIGH, sizey + LOW + HIGH
    vmem = pl.BlockSpec(memory_space=pltpu.VMEM)
    smem = pl.BlockSpec(memory_space=pltpu.SMEM)
    iterate, corr = pl.pallas_call(
        functools.partial(cycle_kernel, nx, ny),
        out_shape=(
            jax.ShapeDtypeStruct((sizex, sizey, 2, 8, nzc), f32),
            jax.ShapeDtypeStruct((cx + 1, cy + 1, 8, nzc), f32),
        ),
        in_specs=[vmem, smem, smem, smem, smem],
        out_specs=(vmem, vmem),
        scratch_shapes=[
            pltpu.VMEM((extx, 2 * exty, nzc), f32),
            pltpu.VMEM((6, extx, 2 * exty, nzc), f32),
            pltpu.VMEM((2, cx + 2, 2 * exty, nzc), f32),
            pltpu.VMEM((extx + exty, 2, 8, nzc), f32),
            pltpu.VMEM((extx, exty, 2, 8, nzc), f32),
            pltpu.VMEM((extx, exty, 2, 8, nzc), f32),
            pltpu.VMEM((extx, exty, 2, 8, nzc), f32),
            pltpu.VMEM((sizex + 1, cy, 8, nzc), f32),
            pltpu.VMEM((cx + 4, cy + 4, 8, nzc), f32),
            pltpu.VMEM((cx + 4, cy + 4, 8, nzc), f32),
            pltpu.VMEM((cx + 4, cy + 4, 8, nzc), f32),
            pltpu.SemaphoreType.DMA((3, len(DIRS))),
            pltpu.SemaphoreType.DMA((3, len(DIRS))),
        ],
        compiler_params=pltpu.CompilerParams(
            collective_id=0, has_side_effects=True, vmem_limit_bytes=24 * 2**20
        ),
    )(labels, eps_r, eps_i, angles, pick)
    return pl.pallas_call(
        prolong_kernel,
        out_shape=jax.ShapeDtypeStruct((2, 4, sizex, sizey, sizez), f32),
        in_specs=[vmem, vmem],
        out_specs=vmem,
        scratch_shapes=[pltpu.VMEM((sizex, 2, 8 * sizey, nzc), f32)],
        compiler_params=pltpu.CompilerParams(vmem_limit_bytes=16 * 2**20),
    )(iterate, corr)


def solution(mesh):
    return jax.shard_map(
        functools.partial(local, mesh.shape["gx"], mesh.shape["gy"]),
        mesh=mesh,
        in_specs=(P("gx", "gy", None), P(), P(), P(), P()),
        out_specs=P(None, None, "gx", "gy", None),
        check_vma=False,
    )
```

time: 151 us -> 24.6 us (0.16); the launches traced: 148 us -> 24.3 us
  starting transfers between devices: 64.9 us -> 0 us
  waiting for transfers between devices: 38.1 us -> 0 us
  other arithmetic: 21.9 us -> 0 us
  Pallas kernels: 0 us -> 20.8 us
  local copies, waits for them, and re-layouts: 22.6 us -> 3.44 us
    ppermute x24 -> x0, starting transfers between devices: 64.9 us -> none  [the longest x10 37.3 us: with_halo(): lax.ppermute(tail, axis, [(i, (i + 1) % count) for i in range(ends)])]
    ppermute x24 -> x0, waiting for transfers between devices: 38.1 us -> none  [the longest x10 25.3 us: with_halo(): lax.ppermute(head, axis, [((i + 1) % count, i) for i in range(ends)])]
    pallas_call x0 -> x2, Pallas kernels: none -> 20.8 us  [the longest x1 19.5 us: local(): pl.pallas_call(functools.partial(cycle_kernel, nx, ny), out_shape=(jax.Sh...]
    slice x19 -> x0, local copies, waits for them, and re-layouts: 11.3 us -> none  [the longest x1 2.2 us: restrict_axis(): high_side = lax.slice_in_dim(values, 2, 2 * planes + 1, 2, along)]
    another operation x8 -> x0, other arithmetic: 10.6 us -> none  [the longest x2 9.99 us: local(): jnp.stack([eps_real + SHIFT_IMAG * eps_imag, eps_imag - SHIFT_IMAG * eps_...]
    another operation x4 -> x0, local copies, waits for them, and re-layouts: 6.46 us -> none  [prolong_axis(): stacked = jnp.stack([even_rows, upper_part], axis=along + 1)]
    reshape x1 -> x0, local copies, waits for them, and re-layouts: 4.33 us -> none  [prolong_axis(): return stacked.reshape(new_shape)]
    sub x17 -> x0, other arithmetic: 4.12 us -> none  [the longest x2 2.77 us: local(): source - apply_operator(iterate, fine_padded(iterate), medium, 1.0)]
  transfers between devices with their start and end apart: 24 -> 0, of which waited for: 14 -> 0; matrix products, arithmetic and copies ran while one was open for 1% -> 0% of each run, Pallas kernels for 0% -> 0%
where the time goes in v1:
time: 24.6 us; the launch traced here: 24.3 us
  Pallas kernels  20.8 us (85%)
  local copies, waits for them, and re-layouts  3.44 us (14%)
    pallas_call x1, Pallas kernels, local(): pl.pallas_call(functools.partial(cycle_kernel, nx, ny), out_shape=(jax.Sh...  19.5 us
    unnamed x10, local copies, waits for them, and re-layouts  3.44 us
    pallas_call x1, Pallas kernels, local(): pl.pallas_call(prolong_kernel, out_shape=jax.ShapeDtypeStruct((2, 4, size...  1.36 us

profile of v1, /device:TPU:1, one launch (start us, length us, event | category | flops | bytes accessed | tf_op | source)
XLA Modules:
  0.0 24.3 jit_solution(14862546327379284148)
XLA Ops:
  0.0 0.0 copy-start
  0.0 0.8 %copy-done = s32[6,8,256]{2,1,0:T(8,128)S(1)} copy-done((s32[6,8,256]{2,1,0:T(8,128)S(1)}, s32[6,8,256]{2,1,0:T(8,128)}, u32[]{:S(2)}) %copy-start) | copy-done | bytes 49176
  0.8 0.0 copy-start.1
  0.8 0.7 %copy-done.1 = f32[360]{0:T(512)S(1)} copy-done((f32[360]{0:T(512)S(1)}, f32[360]{0:T(512)}, u32[]{:S(2)}) %copy-start.1) | copy-done | bytes 1464
  1.5 0.0 copy-start.2
  1.5 0.7 %copy-done.2 = f32[8]{0:T(128)S(1)} copy-done((f32[8]{0:T(128)S(1)}, f32[8]{0:T(128)}, u32[]{:S(2)}) %copy-start.2) | copy-done | bytes 56
  2.1 0.0 copy-start.3
  2.1 0.7 %copy-done.3 = f32[8]{0:T(128)S(1)} copy-done((f32[8]{0:T(128)S(1)}, f32[8]{0:T(128)}, u32[]{:S(2)}) %copy-start.3) | copy-done | bytes 56
  2.8 0.0 copy-start.4
  2.8 0.7 %copy-done.4 = s32[4]{0:T(128)S(1)} copy-done((s32[4]{0:T(128)S(1)}, s32[4]{0:T(128)}, u32[]{:S(2)}) %copy-start.4) | copy-done | bytes 40
  3.4 19.5 %shard_map.55 = (f32[6,8,2,8,128]{4,3,2,1,0:T(8,128)S(1)}, f32[4,5,8,128]{3,2,1,0:T(8,128)S(1)}) custom-call(s32[6,8,256]{2,1,0:T(8,128)S(1)} %copy-done, f32[8]{0:T(128)S(1)} %copy-done.2, f32[8]{0:T(128)S(1)} %copy-done.3, f32[360]{0:T(512)S(1)} %copy-done.1, s32[4]{0:T(128)S(1)} %copy-done.4), custom_call_target="tpu_custom_call" | custom-call | tf_op jit(solution)/shard_map/pallas_call | solution.py:359
  22.9 1.4 %shard_map.56 = f32[2,4,6,8,256]{4,3,2,1,0:T(8,128)} custom-call(f32[6,8,2,8,128]{4,3,2,1,0:T(8,128)S(1)} %get-tuple-element.7.iterate_ref, f32[4,5,8,128]{3,2,1,0:T(8,128)S(1)} %get-tuple-element.8.corr_ref), custom_call_target="tpu_custom_call" | custom-call | tf_op jit(solution)/shard_map/pallas_call | solution.py:386
Async XLA Ops:
  0.0 0.8 %copy-start = (s32[6,8,256]{2,1,0:T(8,128)S(1)}, s32[6,8,256]{2,1,0:T(8,128)}, u32[]{:S(2)}) copy-start(s32[6,8,256]{2,1,0:T(8,128)} %labels_ref.1) | copy-start | bytes 147460
  0.8 0.7 %copy-start.1 = (f32[360]{0:T(512)S(1)}, f32[360]{0:T(512)}, u32[]{:S(2)}) copy-start(f32[360]{0:T(512)} %angles_ref.1) | copy-start | bytes 4324
  1.5 0.7 %copy-start.2 = (f32[8]{0:T(128)S(1)}, f32[8]{0:T(128)}, u32[]{:S(2)}) copy-start(f32[8]{0:T(128)} %eps_r_ref.1) | copy-start | bytes 100
  2.1 0.7 %copy-start.3 = (f32[8]{0:T(128)S(1)}, f32[8]{0:T(128)}, u32[]{:S(2)}) copy-start(f32[8]{0:T(128)} %eps_i_ref.1) | copy-start | bytes 100
  2.8 0.7 %copy-start.4 = (s32[4]{0:T(128)S(1)}, s32[4]{0:T(128)}, u32[]{:S(2)}) copy-start(s32[4]{0:T(128)} %pick_ref.1) | copy-start | bytes 52

commit v2 on v1

--- a/solution.py
+++ b/solution.py
@@ -68,11 +68,22 @@
 
 def cycle_kernel(
     nx, ny,
-    labels_ref, eps_r_ref, eps_i_ref, angles_ref, pick_ref,
+    labels_hbm, eps_r_hbm, eps_i_hbm, angles_hbm, pick_hbm,
     iterate_ref, corr_ref,
+    labels_ref, eps_r_ref, eps_i_ref, angles_ref, pick_ref, load_sems,
     lab, tab, ctab, ewave, wave, it0, w, yz, c0, c1, c2,
-    send_sems, recv_sems,
+    send_sems, recv_sems, plane_sends, plane_recvs, iterate, store_sem,
 ):
+    loads = []
+    for k, (source, target) in enumerate((
+        (labels_hbm, labels_ref),
+        (pick_hbm, pick_ref),
+        (angles_hbm, angles_ref),
+        (eps_r_hbm, eps_r_ref),
+        (eps_i_hbm, eps_i_ref),
+    )):
+        loads.append(pltpu.make_async_copy(source, target, load_sems.at[k]))
+        loads[-1].start()
     sizex, sizey, sizez = labels_ref.shape
     nzc = sizez // 2
     cx, cy = sizex // 2, sizey // 2
@@ -101,6 +112,7 @@
     row = lax.broadcasted_iota(jnp.int32, (sizez, sizez), 0)
     col = lax.broadcasted_iota(jnp.int32, (sizez, sizez), 1)
     split = jnp.where(row == jnp.where(col < nzc, 2 * col, 2 * (col - nzc) + 1), 1.0, 0.0).astype(jnp.bfloat16)
+    loads[0].wait()
     mine = labels_ref[...].astype(f32).reshape(sizex * sizey, sizez).astype(jnp.bfloat16)
     mine = jnp.dot(mine, split, preferred_element_type=f32)
     for x in range(sizex):
@@ -147,6 +159,8 @@
     sign = jnp.where(imag, 1.0, -1.0)
     column = field % 4
     incidence = jnp.zeros((8, nzc), f32)
+    for load in loads[1:]:
+        load.wait()
     for c in range(4):
         incidence = jnp.where(column == c, angles_ref[pick_ref[c]], incidence)
     wavenumber = jnp.sqrt(jnp.full((8, nzc), WAVE_SQUARED, f32))
@@ -215,14 +229,11 @@
                 it0[x, y, half] = bcast(tab, (0, *at)) * wave_one + bcast(tab, (1, *at)) * wave_two
         return carry
 
-    lax.fori_loop(0, extx, fill_start, 0)
 
     def fill_coarse_table(i, carry):
         inside, _, _, med_r, med_i = media(lab[2 * i + LOW - 1])
         ctab[0, i], ctab[1, i] = damped_inverse(inside, med_r, med_i, COARSE_CENTRE)
         return carry
-
-    lax.fori_loop(0, cx + 2, fill_coarse_table, 0)
 
     def times(real, imaginary, values):
         return real * values + imaginary * (sign * pltpu.roll(values, 4, 0))
@@ -234,16 +245,6 @@
                 change = times(bcast(tab, (2, *at)), bcast(tab, (3, *at)), near)
                 w[x, y, half] = (1.0 + 0.2 - DAMPING) * it0[x, y, half] + change
         return carry
-
-    lax.fori_loop(1, extx - 1, sweep, 0)
-
-    def iterate_out(x, carry):
-        for y in range(sizey):
-            for half in (0, 1):
-                iterate_ref[x, y, half] = w[x + LOW, y + LOW, half] + DAMPING * it0[x + LOW, y + LOW, half]
-        return carry
-
-    lax.fori_loop(0, sizex, iterate_out, 0)
 
     def restrict(x, carry):
         in_x = jnp.where(jnp.logical_and(x == LOW + sizex, px == nx - 1), 0.0, 1.0 / 30.0)
@@ -267,8 +268,6 @@
             yz[x - LOW, j] = (even + shift_down(even, last)) + 2.0 * odd
         return carry
 
-    lax.fori_loop(LOW, LOW + sizex + 1, restrict, 0)
-
     def coarse_inverse(i, j):
         at = (i - 1, pl.ds(2 * (2 * (j - 2) + 1 + LOW) + 1, 1))
         return bcast(ctab, (0, *at)), bcast(ctab, (1, *at))
@@ -279,9 +278,50 @@
             c0[i + 2, j + 2] = times(*coarse_inverse(i + 2, j + 2), rhs * (1.0 / 64.0))
         return carry
 
-    lax.fori_loop(0, cx, first_correction, 0)
-    sent_first = exchange(1, c0, (cx, cy), 2, 2, 1)
-    finish(sent_first)
+    def send_plane(i):
+        copies = []
+        for dx in (-1, 1, 0):
+            if (dx < 0 and i >= 2) or (dx > 0 and i < cx - 2):
+                continue
+            to = i + 2 - dx * cx
+            for dy in (-1, 1, 0):
+                if dx == 0 and dy == 0:
+                    continue
+                fy, ty, ly = windows(dy, cy, 2, 2)
+                d = DIRS.index((dx, dy))
+                copy = pltpu.make_async_remote_copy(
+                    src_ref=c0.at[i + 2, pl.ds(fy, ly)],
+                    dst_ref=c0.at[to, pl.ds(ty, ly)],
+                    send_sem=plane_sends.at[i, d],
+                    recv_sem=plane_recvs.at[i, d],
+                    device_id=(px + dx, py + dy),
+                    device_id_type=pl.DeviceIdType.MESH,
+                )
+                pl.when(there(dx, dy))(copy.start)
+                copies.append(((dx, dy), copy))
+        return copies
+
+    lax.fori_loop(0, cx + 2, fill_coarse_table, 0)
+    sent_planes = []
+    for i in range(cx):
+        upto = 2 * i + 7
+        lax.fori_loop(upto - 2 if i else 0, upto, fill_start, 0)
+        lax.fori_loop(upto - 3 if i else 1, upto - 1, sweep, 0)
+        lax.fori_loop(upto - 4 if i else LOW, upto - 2, restrict, 0)
+        first_correction(i, 0)
+        sent_planes += send_plane(i)
+
+    def iterate_out(x, carry):
+        for y in range(sizey):
+            for half in (0, 1):
+                iterate[x, y, half] = w[x + LOW, y + LOW, half] + DAMPING * it0[x + LOW, y + LOW, half]
+        return carry
+
+    lax.fori_loop(0, sizex, iterate_out, 0)
+    store = pltpu.make_async_copy(iterate, iterate_ref, store_sem)
+    store.start()
+    for (dx, dy), copy in sent_planes:
+        pl.when(there(-dx, -dy))(copy.wait_recv)
 
     def coarse_sweep(source, put, i_range, j_range):
         def body(i, carry):
@@ -300,15 +340,24 @@
 
     coarse_sweep(c0, into(c1, 0), (1, cx + 3), range(1, cy + 3))
     coarse_sweep(c1, into(c2, 0), (2, cx + 2), range(2, cy + 2))
-    sent_third = exchange(2, c2, (cx, cy), 2, 1, 1)
+    sent_third = exchange(1, c2, (cx, cy), 2, 1, 1)
     finish(sent_third)
     coarse_sweep(c2, into(corr_ref, 1), (1, cx + 2), range(1, cy + 2))
-    for sent in (sent_labels, sent_first, sent_third):
+    for sent in (sent_labels, sent_third):
         finish_sends(sent)
-
-
-def prolong_kernel(iterate_ref, corr_ref, out_ref, flat):
+    for (dx, dy), copy in sent_planes:
+        pl.when(there(dx, dy))(copy.wait_send)
+    store.wait()
+
+
+def prolong_kernel(iterate_hbm, corr_hbm, out_hbm, iterate_ref, corr_ref, out_ref, flat, load_sems, store_sems):
     sizex, sizey = iterate_ref.shape[:2]
+    loads = [pltpu.make_async_copy(corr_hbm, corr_ref, load_sems.at[sizex])]
+    for x in range(sizex):
+        loads.append(pltpu.make_async_copy(iterate_hbm.at[x], iterate_ref.at[x], load_sems.at[x]))
+    for load in loads:
+        load.start()
+    stores = []
     nzc = iterate_ref.shape[-1]
     sizez = 2 * nzc
     lane = lax.broadcasted_iota(jnp.int32, (8, nzc), 1)
@@ -317,7 +366,9 @@
     col = lax.broadcasted_iota(jnp.int32, (sizez, sizez), 1)
     merge = jnp.where(col == jnp.where(row < nzc, 2 * row, 2 * (row - nzc) + 1), 1.0, 0.0).astype(jnp.bfloat16)
 
+    loads[0].wait()
     for x in range(sizex):
+        loads[x + 1].wait()
         i = x // 2 + 1
         across = {}
         for j in range(sizey // 2 + 1):
@@ -344,9 +395,13 @@
             flat[x, half] = merged[:, half * nzc : (half + 1) * nzc]
         for f in range(8):
             for half in (0, 1):
-                out_ref[f // 4, f % 4, x, :, half * nzc : (half + 1) * nzc] = flat[
+                out_ref[x, f // 4, f % 4, :, half * nzc : (half + 1) * nzc] = flat[
                     x, half, pl.ds(f, sizey, stride=8), :
                 ]
+        stores.append(pltpu.make_async_copy(out_ref.at[x], out_hbm.at[:, :, x], store_sems.at[x]))
+        stores[-1].start()
+    for store in stores:
+        store.wait()
 
 
 def local(nx, ny, labels, eps_r, eps_i, angles, pick):
@@ -355,16 +410,22 @@
     cx, cy = sizex // 2, sizey // 2
     extx, exty = sizex + LOW + HIGH, sizey + LOW + HIGH
     vmem = pl.BlockSpec(memory_space=pltpu.VMEM)
-    smem = pl.BlockSpec(memory_space=pltpu.SMEM)
+    hbm = pl.BlockSpec(memory_space=pltpu.HBM)
     iterate, corr = pl.pallas_call(
         functools.partial(cycle_kernel, nx, ny),
         out_shape=(
             jax.ShapeDtypeStruct((sizex, sizey, 2, 8, nzc), f32),
             jax.ShapeDtypeStruct((cx + 1, cy + 1, 8, nzc), f32),
         ),
-        in_specs=[vmem, smem, smem, smem, smem],
-        out_specs=(vmem, vmem),
+        in_specs=[hbm] * 5,
+        out_specs=(hbm, vmem),
         scratch_shapes=[
+            pltpu.VMEM(labels.shape, jnp.int32),
+            pltpu.SMEM(eps_r.shape, f32),
+            pltpu.SMEM(eps_i.shape, f32),
+            pltpu.SMEM(angles.shape, f32),
+            pltpu.SMEM(pick.shape, jnp.int32),
+            pltpu.SemaphoreType.DMA((5,)),
             pltpu.VMEM((extx, 2 * exty, nzc), f32),
             pltpu.VMEM((6, extx, 2 * exty, nzc), f32),
             pltpu.VMEM((2, cx + 2, 2 * exty, nzc), f32),
@@ -376,20 +437,31 @@
             pltpu.VMEM((cx + 4, cy + 4, 8, nzc), f32),
             pltpu.VMEM((cx + 4, cy + 4, 8, nzc), f32),
             pltpu.VMEM((cx + 4, cy + 4, 8, nzc), f32),
-            pltpu.SemaphoreType.DMA((3, len(DIRS))),
-            pltpu.SemaphoreType.DMA((3, len(DIRS))),
+            pltpu.SemaphoreType.DMA((2, len(DIRS))),
+            pltpu.SemaphoreType.DMA((2, len(DIRS))),
+            pltpu.SemaphoreType.DMA((cx, len(DIRS))),
+            pltpu.SemaphoreType.DMA((cx, len(DIRS))),
+            pltpu.VMEM((sizex, sizey, 2, 8, nzc), f32),
+            pltpu.SemaphoreType.DMA,
         ],
         compiler_params=pltpu.CompilerParams(
-            collective_id=0, has_side_effects=True, vmem_limit_bytes=24 * 2**20
+            collective_id=0, has_side_effects=True, vmem_limit_bytes=60 * 2**20
         ),
     )(labels, eps_r, eps_i, angles, pick)
     return pl.pallas_call(
         prolong_kernel,
         out_shape=jax.ShapeDtypeStruct((2, 4, sizex, sizey, sizez), f32),
-        in_specs=[vmem, vmem],
-        out_specs=vmem,
-        scratch_shapes=[pltpu.VMEM((sizex, 2, 8 * sizey, nzc), f32)],
-        compiler_params=pltpu.CompilerParams(vmem_limit_bytes=16 * 2**20),
+        in_specs=[hbm, hbm],
+        out_specs=hbm,
+        scratch_shapes=[
+            pltpu.VMEM((sizex, sizey, 2, 8, nzc), f32),
+            pltpu.VMEM((cx + 1, cy + 1, 8, nzc), f32),
+            pltpu.VMEM((sizex, 2, 4, sizey, sizez), f32),
+            pltpu.VMEM((sizex, 2, 8 * sizey, nzc), f32),
+            pltpu.SemaphoreType.DMA((sizex + 1,)),
+            pltpu.SemaphoreType.DMA((sizex,)),
+        ],
+        compiler_params=pltpu.CompilerParams(vmem_limit_bytes=60 * 2**20),
     )(iterate, corr)
 
 

time: 24.6 us -> 22.7 us (0.923)
  local copies, waits for them, and re-layouts: 3.44 us -> 0 us
  Pallas kernels: 20.8 us -> 22.5 us
    unnamed x10 -> x0, local copies, waits for them, and re-layouts: 3.44 us -> none
    pallas_call x1, Pallas kernels: 1.36 us -> 3.42 us  [local(): pl.pallas_call(prolong_kernel, out_shape=jax.ShapeDtypeStruct((2, 4, size...]
    pallas_call x1, Pallas kernels: 19.5 us -> 19.1 us  [local(): pl.pallas_call(functools.partial(cycle_kernel, nx, ny), out_shape=(jax.Sh...]
where the time goes in v2:
time: 22.7 us; the launch traced here: 22.5 us
  Pallas kernels  22.5 us (99%)
    pallas_call x1, Pallas kernels, local(): pl.pallas_call(functools.partial(cycle_kernel, nx, ny), out_shape=(jax.Sh...  19.1 us
    pallas_call x1, Pallas kernels, local(): pl.pallas_call(prolong_kernel, out_shape=jax.ShapeDtypeStruct((2, 4, size...  3.42 us

profile of v2, /device:TPU:1, one launch (start us, length us, event | category | flops | bytes accessed | tf_op | source)
XLA Modules:
  0.0 22.5 jit_solution(11167355983285707659)
XLA Ops:
  0.0 19.1 %shard_map.55 = (f32[6,8,2,8,128]{4,3,2,1,0:T(8,128)}, f32[4,5,8,128]{3,2,1,0:T(8,128)}) custom-call(s32[6,8,256]{2,1,0:T(8,128)} %labels_hbm.1, f32[8]{0:T(128)} %eps_r_hbm.1, f32[8]{0:T(128)} %eps_i_hbm.1, f32[360]{0:T(512)} %angles_hbm.1, s32[4]{0:T(128)} %pick_hbm.1), custom_call_target="tpu_custom_call" | custom-call | tf_op jit(solution)/shard_map/pallas_call | solution.py:414
  19.1 3.4 %shard_map.56 = f32[2,4,6,8,256]{4,3,2,1,0:T(8,128)} custom-call(f32[6,8,2,8,128]{4,3,2,1,0:T(8,128)} %get-tuple-element.7.iterate_hbm, f32[4,5,8,128]{3,2,1,0:T(8,128)} %get-tuple-element.8.corr_hbm), custom_call_target="tpu_custom_call" | custom-call | tf_op jit(solution)/shard_map/pallas_call | solution.py:451

commit v3 on v2

--- a/solution.py
+++ b/solution.py
@@ -15,7 +15,7 @@
 CENTRE = 128.0 / 30.0
 COARSE_CENTRE = 128.0 / 120.0
 LOW, HIGH = 2, 3
-DIRS = [(dx, dy) for dx in (-1, 0, 1) for dy in (-1, 0, 1) if (dx, dy) != (0, 0)]
+DIRS = [(-1, 0), (1, 0), (-1, -1), (1, 1), (-1, 1), (1, -1), (0, -1), (0, 1)]
 f32 = jnp.float32
 
 
@@ -72,7 +72,7 @@
     iterate_ref, corr_ref,
     labels_ref, eps_r_ref, eps_i_ref, angles_ref, pick_ref, load_sems,
     lab, tab, ctab, ewave, wave, it0, w, yz, c0, c1, c2,
-    send_sems, recv_sems, plane_sends, plane_recvs, iterate, store_sem,
+    send_sems, recv_sems, plane_sends, plane_recvs,
 ):
     loads = []
     for k, (source, target) in enumerate((
@@ -314,12 +314,10 @@
     def iterate_out(x, carry):
         for y in range(sizey):
             for half in (0, 1):
-                iterate[x, y, half] = w[x + LOW, y + LOW, half] + DAMPING * it0[x + LOW, y + LOW, half]
+                iterate_ref[x, y, half] = w[x + LOW, y + LOW, half] + DAMPING * it0[x + LOW, y + LOW, half]
         return carry
 
     lax.fori_loop(0, sizex, iterate_out, 0)
-    store = pltpu.make_async_copy(iterate, iterate_ref, store_sem)
-    store.start()
     for (dx, dy), copy in sent_planes:
         pl.when(there(-dx, -dy))(copy.wait_recv)
 
@@ -347,16 +345,10 @@
         finish_sends(sent)
     for (dx, dy), copy in sent_planes:
         pl.when(there(dx, dy))(copy.wait_send)
-    store.wait()
-
-
-def prolong_kernel(iterate_hbm, corr_hbm, out_hbm, iterate_ref, corr_ref, out_ref, flat, load_sems, store_sems):
+
+
+def prolong_kernel(iterate_ref, corr_ref, out_hbm, out_ref, flat, store_sems):
     sizex, sizey = iterate_ref.shape[:2]
-    loads = [pltpu.make_async_copy(corr_hbm, corr_ref, load_sems.at[sizex])]
-    for x in range(sizex):
-        loads.append(pltpu.make_async_copy(iterate_hbm.at[x], iterate_ref.at[x], load_sems.at[x]))
-    for load in loads:
-        load.start()
     stores = []
     nzc = iterate_ref.shape[-1]
     sizez = 2 * nzc
@@ -366,9 +358,7 @@
     col = lax.broadcasted_iota(jnp.int32, (sizez, sizez), 1)
     merge = jnp.where(col == jnp.where(row < nzc, 2 * row, 2 * (row - nzc) + 1), 1.0, 0.0).astype(jnp.bfloat16)
 
-    loads[0].wait()
     for x in range(sizex):
-        loads[x + 1].wait()
         i = x // 2 + 1
         across = {}
         for j in range(sizey // 2 + 1):
@@ -418,7 +408,7 @@
             jax.ShapeDtypeStruct((cx + 1, cy + 1, 8, nzc), f32),
         ),
         in_specs=[hbm] * 5,
-        out_specs=(hbm, vmem),
+        out_specs=(vmem, vmem),
         scratch_shapes=[
             pltpu.VMEM(labels.shape, jnp.int32),
             pltpu.SMEM(eps_r.shape, f32),
@@ -441,27 +431,22 @@
             pltpu.SemaphoreType.DMA((2, len(DIRS))),
             pltpu.SemaphoreType.DMA((cx, len(DIRS))),
             pltpu.SemaphoreType.DMA((cx, len(DIRS))),
-            pltpu.VMEM((sizex, sizey, 2, 8, nzc), f32),
-            pltpu.SemaphoreType.DMA,
         ],
         compiler_params=pltpu.CompilerParams(
-            collective_id=0, has_side_effects=True, vmem_limit_bytes=60 * 2**20
+            collective_id=0, has_side_effects=True, vmem_limit_bytes=24 * 2**20
         ),
-    )(labels, eps_r, eps_i, angles, pick)
+    )(*(pltpu.with_memory_space_constraint(v, pltpu.HBM) for v in (labels, eps_r, eps_i, angles, pick)))
     return pl.pallas_call(
         prolong_kernel,
         out_shape=jax.ShapeDtypeStruct((2, 4, sizex, sizey, sizez), f32),
-        in_specs=[hbm, hbm],
+        in_specs=[vmem, vmem],
         out_specs=hbm,
         scratch_shapes=[
-            pltpu.VMEM((sizex, sizey, 2, 8, nzc), f32),
-            pltpu.VMEM((cx + 1, cy + 1, 8, nzc), f32),
             pltpu.VMEM((sizex, 2, 4, sizey, sizez), f32),
             pltpu.VMEM((sizex, 2, 8 * sizey, nzc), f32),
-            pltpu.SemaphoreType.DMA((sizex + 1,)),
             pltpu.SemaphoreType.DMA((sizex,)),
         ],
-        compiler_params=pltpu.CompilerParams(vmem_limit_bytes=60 * 2**20),
+        compiler_params=pltpu.CompilerParams(vmem_limit_bytes=24 * 2**20),
     )(iterate, corr)
 
 

time: 22.7 us -> 20.1 us (0.89)
  Pallas kernels: 22.5 us -> 19.9 us
    pallas_call x1, Pallas kernels: 3.42 us -> 1.32 us  [local(): pl.pallas_call(prolong_kernel, out_shape=jax.ShapeDtypeStruct((2, 4, size...]
    pallas_call x1, Pallas kernels: 19.1 us -> 18.6 us  [local(): pl.pallas_call(functools.partial(cycle_kernel, nx, ny), out_shape=(jax.Sh...]
where the time goes in v3:
time: 20.1 us; the launch traced here: 19.9 us
  Pallas kernels  19.9 us (99%)
    pallas_call x1, Pallas kernels, local(): pl.pallas_call(functools.partial(cycle_kernel, nx, ny), out_shape=(jax.Sh...  18.6 us
    pallas_call x1, Pallas kernels, local(): pl.pallas_call(prolong_kernel, out_shape=jax.ShapeDtypeStruct((2, 4, size...  1.32 us

profile of v3, /device:TPU:1, one launch (start us, length us, event | category | flops | bytes accessed | tf_op | source)
XLA Modules:
  0.0 19.9 jit_solution(15481115824884488720)
XLA Ops:
  0.0 18.6 %shard_map.55 = (f32[6,8,2,8,128]{4,3,2,1,0:T(8,128)S(1)}, f32[4,5,8,128]{3,2,1,0:T(8,128)S(1)}) custom-call(s32[6,8,256]{2,1,0:T(8,128)} %labels_hbm.1, f32[8]{0:T(128)} %eps_r_hbm.1, f32[8]{0:T(128)} %eps_i_hbm.1, f32[360]{0:T(512)} %angles_hbm.1, s32[4]{0:T(128)} %pick_hbm.1), custom_call_target="tpu_custom_call" | custom-call | tf_op jit(solution)/shard_map/pallas_call | solution.py:404
  18.6 1.3 %shard_map.56 = f32[2,4,6,8,256]{4,3,2,1,0:T(8,128)} custom-call(f32[6,8,2,8,128]{4,3,2,1,0:T(8,128)S(1)} %get-tuple-element.7.iterate_ref, f32[4,5,8,128]{3,2,1,0:T(8,128)S(1)} %get-tuple-element.8.corr_ref), custom_call_target="tpu_custom_call" | custom-call | tf_op jit(solution)/shard_map/pallas_call | solution.py:439

commit v4 on v3

--- a/solution.py
+++ b/solution.py
@@ -72,7 +72,7 @@
     iterate_ref, corr_ref,
     labels_ref, eps_r_ref, eps_i_ref, angles_ref, pick_ref, load_sems,
     lab, tab, ctab, ewave, wave, it0, w, yz, c0, c1, c2,
-    send_sems, recv_sems, plane_sends, plane_recvs,
+    send_sems, recv_sems, plane_sends, plane_recvs, own, otab,
 ):
     loads = []
     for k, (source, target) in enumerate((
@@ -117,9 +117,9 @@
     mine = jnp.dot(mine, split, preferred_element_type=f32)
     for x in range(sizex):
         for half in (0, 1):
-            lab[x + LOW, pl.ds(2 * LOW + half, sizey, stride=2), :] = mine[
-                x * sizey : (x + 1) * sizey, half * nzc : (half + 1) * nzc
-            ]
+            piece = mine[x * sizey : (x + 1) * sizey, half * nzc : (half + 1) * nzc]
+            lab[x + LOW, pl.ds(2 * LOW + half, sizey, stride=2), :] = piece
+            own[x, pl.ds(half, sizey, stride=2), :] = piece
 
     def exchange(phase, buf, sizes, low, high, fold):
         copies = []
@@ -190,7 +190,6 @@
 
     lax.fori_loop(0, extx, fill_wave, 0)
     eps_table = [(eps_r_ref[m], eps_i_ref[m]) for m in range(MAT)]
-    finish(sent_labels)
 
     def media(label):
         eps_r = jnp.zeros(label.shape, f32)
@@ -211,24 +210,39 @@
     def bcast(ref, at):
         return jnp.broadcast_to(ref[at], (8, nzc))
 
-    def fill_start(x, carry):
-        inside, eps_r, eps_i, med_r, med_i = media(lab[x])
-        inv_r, inv_i = damped_inverse(inside, med_r, med_i, CENTRE)
-        src_r = jnp.where(inside, SOURCE_GAIN * (eps_r - 1.0), 0.0)
-        src_i = SOURCE_GAIN * eps_i
-        tab[0, x] = inv_r * src_r - inv_i * src_i
-        tab[1, x] = inv_r * src_i + inv_i * src_r
-        tab[2, x] = inv_r * (1.0 / 30.0)
-        tab[3, x] = inv_i * (1.0 / 30.0)
-        tab[4, x] = (0.2 * (1.0 - DAMPING)) * src_r
-        tab[5, x] = (0.2 * (1.0 - DAMPING)) * src_i
-        for y in range(exty):
-            wave_one, wave_two = wave[x, y, 0], wave[x, y, 1]
-            for half in (0, 1):
-                at = (x, pl.ds(2 * y + half, 1))
-                it0[x, y, half] = bcast(tab, (0, *at)) * wave_one + bcast(tab, (1, *at)) * wave_two
-        return carry
-
+    def start_body(labels_at, table, rows, off):
+        def body(x, carry):
+            at_x = x - off
+            inside, eps_r, eps_i, med_r, med_i = media(labels_at[at_x])
+            inv_r, inv_i = damped_inverse(inside, med_r, med_i, CENTRE)
+            src_r = jnp.where(inside, SOURCE_GAIN * (eps_r - 1.0), 0.0)
+            src_i = SOURCE_GAIN * eps_i
+            table[0, at_x] = inv_r * src_r - inv_i * src_i
+            table[1, at_x] = inv_r * src_i + inv_i * src_r
+            table[2, at_x] = inv_r * (1.0 / 30.0)
+            table[3, at_x] = inv_i * (1.0 / 30.0)
+            if off == 0:
+                table[4, at_x] = (0.2 * (1.0 - DAMPING)) * src_r
+                table[5, at_x] = (0.2 * (1.0 - DAMPING)) * src_i
+            for y in rows:
+                wave_one, wave_two = wave[x, y, 0], wave[x, y, 1]
+                for half in (0, 1):
+                    at = (at_x, pl.ds(2 * (y - off) + half, 1))
+                    it0[x, y, half] = (
+                        bcast(table, (0, *at)) * wave_one + bcast(table, (1, *at)) * wave_two
+                    )
+            return carry
+
+        return body
+
+    def run(low, high, own_low, own_high, rim_body, own_body):
+        for a, b, body in (
+            (low, min(high, own_low), rim_body),
+            (max(low, own_low), min(high, own_high), own_body),
+            (max(low, own_high), high, rim_body),
+        ):
+            if a < b:
+                lax.fori_loop(a, b, body, 0)
 
     def fill_coarse_table(i, carry):
         inside, _, _, med_r, med_i = media(lab[2 * i + LOW - 1])
@@ -238,13 +252,26 @@
     def times(real, imaginary, values):
         return real * values + imaginary * (sign * pltpu.roll(values, 4, 0))
 
-    def sweep(x, carry):
-        for y, even, odd in fine_neighbours(it0, x, range(1, exty - 1), first, last):
-            for half, near in enumerate((even, odd)):
-                at = (x, pl.ds(2 * y + half, 1))
-                change = times(bcast(tab, (2, *at)), bcast(tab, (3, *at)), near)
-                w[x, y, half] = (1.0 + 0.2 - DAMPING) * it0[x, y, half] + change
-        return carry
+    def sweep_body(groups, table, off):
+        def body(x, carry):
+            for rows in groups:
+                for y, even, odd in fine_neighbours(it0, x, rows, first, last):
+                    for half, near in enumerate((even, odd)):
+                        at = (x - off, pl.ds(2 * (y - off) + half, 1))
+                        change = times(bcast(table, (2, *at)), bcast(table, (3, *at)), near)
+                        w[x, y, half] = (1.0 + 0.2 - DAMPING) * it0[x, y, half] + change
+            return carry
+
+        return body
+
+    endx, endy = LOW + sizex, LOW + sizey
+    lax.fori_loop(LOW, endx, start_body(own, otab, range(LOW, endy), LOW), 0)
+    lax.fori_loop(LOW + 1, endx - 1, sweep_body([range(LOW + 1, endy - 1)], otab, LOW), 0)
+    finish(sent_labels)
+    start_rim = start_body(lab, tab, range(exty), 0)
+    start_own = start_body(lab, tab, [*range(LOW), *range(endy, exty)], 0)
+    sweep_rim = sweep_body([range(1, exty - 1)], tab, 0)
+    sweep_own = sweep_body([range(1, LOW + 1), range(endy - 1, exty - 1)], tab, 0)
 
     def restrict(x, carry):
         in_x = jnp.where(jnp.logical_and(x == LOW + sizex, px == nx - 1), 0.0, 1.0 / 30.0)
@@ -301,15 +328,17 @@
                 copies.append(((dx, dy), copy))
         return copies
 
-    lax.fori_loop(0, cx + 2, fill_coarse_table, 0)
     sent_planes = []
     for i in range(cx):
         upto = 2 * i + 7
-        lax.fori_loop(upto - 2 if i else 0, upto, fill_start, 0)
-        lax.fori_loop(upto - 3 if i else 1, upto - 1, sweep, 0)
+        fill_coarse_table(i + 1, 0)
+        run(upto - 2 if i else 0, upto, LOW, endx, start_rim, start_own)
+        run(upto - 3 if i else 1, upto - 1, LOW + 1, endx - 1, sweep_rim, sweep_own)
         lax.fori_loop(upto - 4 if i else LOW, upto - 2, restrict, 0)
         first_correction(i, 0)
         sent_planes += send_plane(i)
+    fill_coarse_table(0, 0)
+    fill_coarse_table(cx + 1, 0)
 
     def iterate_out(x, carry):
         for y in range(sizey):
@@ -431,6 +460,8 @@
             pltpu.SemaphoreType.DMA((2, len(DIRS))),
             pltpu.SemaphoreType.DMA((cx, len(DIRS))),
             pltpu.SemaphoreType.DMA((cx, len(DIRS))),
+            pltpu.VMEM((sizex, 2 * sizey, nzc), f32),
+            pltpu.VMEM((4, sizex, 2 * sizey, nzc), f32),
         ],
         compiler_params=pltpu.CompilerParams(
             collective_id=0, has_side_effects=True, vmem_limit_bytes=24 * 2**20

time: 20.1 us -> 19.9 us (0.990)
    pallas_call x1, Pallas kernels: 18.6 us -> 18.4 us  [local(): pl.pallas_call(functools.partial(cycle_kernel, nx, ny), out_shape=(jax.Sh...]
where the time goes in v4:
time: 19.9 us; the launch traced here: 19.7 us
  Pallas kernels  19.7 us (99%)
    pallas_call x1, Pallas kernels, local(): pl.pallas_call(functools.partial(cycle_kernel, nx, ny), out_shape=(jax.Sh...  18.4 us
    pallas_call x1, Pallas kernels, local(): pl.pallas_call(prolong_kernel, out_shape=jax.ShapeDtypeStruct((2, 4, size...  1.32 us

profile of v4, /device:TPU:1, one launch (start us, length us, event | category | flops | bytes accessed | tf_op | source)
XLA Modules:
  0.0 19.7 jit_solution(7262116375257825721)
XLA Ops:
  0.0 18.4 %shard_map.55 = (f32[6,8,2,8,128]{4,3,2,1,0:T(8,128)S(1)}, f32[4,5,8,128]{3,2,1,0:T(8,128)S(1)}) custom-call(s32[6,8,256]{2,1,0:T(8,128)} %labels_hbm.1, f32[8]{0:T(128)} %eps_r_hbm.1, f32[8]{0:T(128)} %eps_i_hbm.1, f32[360]{0:T(512)} %angles_hbm.1, s32[4]{0:T(128)} %pick_hbm.1), custom_call_target="tpu_custom_call" | custom-call | tf_op jit(solution)/shard_map/pallas_call | solution.py:433
  18.4 1.3 %shard_map.56 = f32[2,4,6,8,256]{4,3,2,1,0:T(8,128)} custom-call(f32[6,8,2,8,128]{4,3,2,1,0:T(8,128)S(1)} %get-tuple-element.7.iterate_ref, f32[4,5,8,128]{3,2,1,0:T(8,128)S(1)} %get-tuple-element.8.corr_ref), custom_call_target="tpu_custom_call" | custom-call | tf_op jit(solution)/shard_map/pallas_call | solution.py:470
